TPU v7x, 512 devices: a whole 4x8x8 slice. The times are simulated.
512 devices in a mesh: group: 8 (over y), fsdp: 8 (over z_lo, core), tp: 8 (over z_hi, x).
Axes of the slice: x: 4, y: 8, z: 8 (z_hi: 2, z_lo: 4; z = z_hi * 4 + z_lo), core: 2. Of those that a mesh axis runs over, the one named last changes fastest.
Arguments:
- hidden_in: bfloat16 [3072, 4, 5120], P(('group', 'fsdp'), None, 'tp'), may hold values from -6 to 6
- norm_gain: bfloat16 [5120], P('tp'), may hold values from 0.099609375 to 1.8984375
- master_query: float32 [5120, 8, 1024], P('fsdp', 'tp', 'group')
- query_gain: float32 [128], replicated, may hold values from 0.1 to 1.9
- kv_cache: bfloat16 [3072, 8, 128, 256], P(('group', 'fsdp'), 'tp'), may hold values from -6 to 6
- lengths: int32 [3072], P(('group', 'fsdp')), may hold values from 4 to 128, as said below
Outputs:
- attended: bfloat16 [3072, 4, 8192], P(('group', 'fsdp'), None, 'tp')
Inputs may be any that keep to these rules, and one draw needn't show every extreme that they name: `lengths`: some row has length 128.
All inputs are finite; a program needn't handle non-finite values.
Results may differ from a plain program's by a relative error of at most 0.035.
Values may be sent and summed in bfloat16 or wider, within the bound.
A program may use at most 64 MiB of HBM per device.

v0:
```python
import jax
import jax.numpy as jnp
from jax import lax
from jax.sharding import PartitionSpec as P

HD = 128
BLK = 128


epsilon = 1e-06


def quantize(master):
    depth, groups_local, columns = master.shape
    blocks = master.reshape(depth // BLK, BLK, groups_local, columns // HD, HD)
    largest = jnp.max(jnp.abs(blocks), axis=(1, 4))
    scales = ((largest + epsilon) / 127.0).astype(jnp.bfloat16)
    levels = jnp.floor(blocks / scales.astype(jnp.float32)[:, None, :, :, None] + 0.5).astype(
        jnp.bfloat16
    )
    return (levels, scales[:, None, :, :])


def accumulate(running, token_blocks, level_stack, scale_stack):
    token_count = running.shape[0]
    groups_local = running.shape[1]
    head_count = running.shape[2]

    def add_block(partial_sum, element):
        token_rows, level_piece, scale_piece = element
        product = jnp.dot(
            token_rows,
            level_piece.reshape(BLK, groups_local * head_count * HD),
            preferred_element_type=jnp.float32,
        )
        product = (
            product.reshape(token_count, groups_local, head_count, HD)
            * scale_piece[0].astype(jnp.float32)[None, :, :, None]
        )
        return (partial_sum + product, None)

    result, unused = lax.scan(add_block, running, (token_blocks, level_stack, scale_stack))
    return result


def rotate(queries, positions):
    half_width = HD // 2
    frequency = jnp.power(1000000.0, -jnp.arange(half_width, dtype=jnp.float32) * (2.0 / HD))
    angles = positions.astype(jnp.float32)[:, :, None] * frequency[None, None, :]
    cosine = jnp.cos(angles)[:, :, None, None, :]
    sine_part = jnp.sin(angles)[:, :, None, None, :]
    front_half = queries[..., :half_width]
    back_half = queries[..., half_width:]
    return jnp.concatenate(
        [front_half * cosine - back_half * sine_part, back_half * cosine + front_half * sine_part],
        axis=-1,
    )


def shards(hidden_in, norm_gain, master_query, query_gain, kv_cache, lengths):
    row_count, step_count, width_part = hidden_in.shape
    token_count = row_count * step_count
    gathered, gain_all = (
        lax.all_gather(hidden_in, "tp", axis=2, tiled=True),
        lax.all_gather(norm_gain, "tp", axis=0, tiled=True),
    )
    floats = gathered.astype(jnp.float32)
    mean_square = jnp.mean(floats * floats, axis=-1, keepdims=True)
    normed = (floats * lax.rsqrt(mean_square + epsilon) * gain_all.astype(jnp.float32)).astype(
        jnp.bfloat16
    )
    width_full = normed.shape[2]
    token_blocks = normed.reshape(token_count, width_full // BLK, BLK).transpose(1, 0, 2)
    levels, scales = quantize(master_query)
    groups_local = levels.shape[2]
    level_heads, scale_heads = (
        lax.all_gather(levels, "group", axis=3, tiled=True),
        lax.all_gather(scales, "group", axis=3, tiled=True),
    )
    head_count = level_heads.shape[3]
    start_sum = jnp.zeros((token_count, groups_local, head_count, HD), jnp.float32)
    queries = accumulate(
        start_sum,
        token_blocks,
        lax.all_gather(level_heads, "fsdp", axis=0, tiled=True),
        lax.all_gather(scale_heads, "fsdp", axis=0, tiled=True),
    )
    queries = queries.reshape(row_count, step_count, groups_local, -1, HD)
    mean_query = jnp.mean(queries * queries, axis=-1, keepdims=True)
    queries = queries * lax.rsqrt(mean_query + epsilon) * query_gain
    positions = lengths[:, None] - step_count + jnp.arange(step_count, dtype=jnp.int32)[None, :]
    scaled = (rotate(queries, positions) * HD ** (-0.5)).astype(jnp.bfloat16)
    cache_keys = kv_cache[..., :HD]
    cache_values = kv_cache[..., HD:]
    scores = jnp.einsum("rskgd,rkjd->rskgj", scaled, cache_keys, preferred_element_type=jnp.float32)
    visible = (
        jnp.arange(kv_cache.shape[2], dtype=jnp.int32)[None, None, None, None, :]
        <= positions[:, :, None, None, None]
    )
    scores = jnp.where(visible, scores, -jnp.inf)
    highest = jnp.max(scores, axis=-1, keepdims=True)
    raised = jnp.exp(scores - highest)
    weights = (raised / jnp.sum(raised, axis=-1, keepdims=True)).astype(jnp.bfloat16)
    result = jnp.einsum(
        "rskgj,rkjd->rskgd", weights, cache_values, preferred_element_type=jnp.float32
    )
    return result.astype(jnp.bfloat16).reshape(row_count, step_count, -1)


def solution(mesh):
    in_specs = (
        P(("group", "fsdp"), None, "tp"),
        P("tp"),
        P("fsdp", "tp", "group"),
        P(),
        P(("group", "fsdp"), "tp", None, None),
        P(("group", "fsdp")),
    )
    out_specs = P(("group", "fsdp"), None, "tp")
    return jax.shard_map(shards, mesh=mesh, in_specs=in_specs, out_specs=out_specs, check_vma=False)
```

profile of v0, /device:TPU:6, one launch (start us, length us, event | category | flops | bytes accessed | tf_op | source)
XLA Modules:
  0.0 335.5 jit_solution(17672108422911601463)
XLA Ops:
  6.5 2.2 abs_reduce_fusion
  8.9 1.8 fusion.23
  10.7 0.7 all-gather.5.cloned.1.call-update
  11.5 45.7 %all-gather.7.cloned.1.call-done = bf16[5,128,1,8,128]{4,1,2,0,3:T(8,128)(2,1)} async-done(((bf16[5,128,1,1,128]{4,1,2,0,3:T(8,128)(2,1)}), bf16[5,128,1,8,128]{4,1,2,0,3:T(8,128)(2,1)}) %all-gather.7.cloned.1.call-update) | async-done | bytes 1310736 | tf_op jit(solution)/shard_map/all_gather | solution.py:77
  57.2 14.9 %all_gather.22 = bf16[5,1,1,8]{0,2,1,3:T(2,128)(2,1)S(1)} all-gather(bf16[5,1,1,1]{0,2,1,3:T(2,128)(2,1)S(1)} %get-tuple-element.102), channel_id=1, replica_groups=mesh['group'=8,'fsdp'=8,'tp'=8] {'group'}, dimensions={3}, use_global_device_ids=true | all-gather | bytes 90 | tf_op jit(solution)/shard_map/all_gather | solution.py:78
  72.1 0.7 reshape.257
  72.8 46.1 %all-gather = bf16[8,1,640]{2,1,0:T(2,128)(2,1)S(1)} all-gather(bf16[1,1,640]{2,1,0:T(2,128)(2,1)S(1)} %reshape.257), channel_id=1, replica_groups=mesh['group'=8,'fsdp'=8,'tp'=8] {'tp'}, dimensions={0}, use_global_device_ids=true | all-gather | bytes 11520 | tf_op jit(solution)/shard_map/all_gather | solution.py:65
  119.0 14.6 %all_gather.23 = bf16[40,1,1,8]{3,2,1,0:T(2,128)(2,1)S(1)} all-gather(bf16[5,1,1,8]{3,2,1,0:T(2,128)(2,1)S(1)} %copy.58), channel_id=1, replica_groups=mesh['group'=8,'fsdp'=8,'tp'=8] {'fsdp'}, dimensions={0}, use_global_device_ids=true | all-gather | bytes 720 | tf_op jit(solution)/shard_map/all_gather | solution.py:86
  133.6 0.7 broadcast_add_fusion
  134.5 0.8 multiply_cosine_fusion
  135.3 8.2 %all-gather.5.cloned.1.call-done = bf16[48,4,5120]{2,1,0:T(4,128)(2,1)} async-done(((bf16[48,4,640]{2,1,0:T(4,128)(2,1)}), bf16[48,4,5120]{2,1,0:T(4,128)(2,1)}) %all-gather.5.cloned.1.call-update) | async-done | bytes 1966096 | tf_op jit(solution)/shard_map/all_gather | solution.py:64
  143.5 2.8 fusion.8
  146.3 1.1 fusion.10
  147.4 2.2 reshape.249
  149.6 2.0 copy.59
  151.6 107.0 %all-gather.9.cloned.1.call-done = bf16[40,128,1,8,128]{4,1,2,0,3:T(8,128)(2,1)} async-done(((bf16[5,128,1,8,128]{4,1,2,0,3:T(8,128)(2,1)}), bf16[40,128,1,8,128]{4,1,2,0,3:T(8,128)(2,1)}) %all-gather.9.cloned.1.call-update) | async-done | bytes 10485776 | tf_op jit(solution)/shard_map/all_gather | solution.py:85
  258.7 64.3 %while.11 = (s32[]{:T(128)}, f32[192,1,8,128]{3,0,2,1:T(8,128)S(1)}, bf16[40,192,128]{2,1,0:T(8,128)(2,1)S(1)}, bf16[40,128,1,8,128]{4,1,2,0,3:T(8,128)(2,1)}, b...) while((s32[]{:T(128)}, f32[192,1,8,128]{3,0,2,1:T(8,128)S(1)}, ...), condition=%wide.region_4.5_spmd.clone, body=%wide.region_3.4_spmd.clone.sunk | while | flops 50921480 | bytes 2933395 | solution.py:42
  258.7 1.0 constant_dynamic-slice_fusion.3
  260.3 1.0 constant_dynamic-slice_fusion.3
  261.9 1.0 constant_dynamic-slice_fusion.3
  263.5 1.0 constant_dynamic-slice_fusion.3
  265.1 1.0 constant_dynamic-slice_fusion.3
  266.7 1.0 constant_dynamic-slice_fusion.3
  268.3 1.0 constant_dynamic-slice_fusion.3
  269.9 1.0 constant_dynamic-slice_fusion.3
  271.5 1.0 constant_dynamic-slice_fusion.3
  273.1 1.0 constant_dynamic-slice_fusion.3
  274.8 1.0 constant_dynamic-slice_fusion.3
  276.4 1.0 constant_dynamic-slice_fusion.3
  278.0 1.0 constant_dynamic-slice_fusion.3
  279.6 1.0 constant_dynamic-slice_fusion.3
  281.2 1.0 constant_dynamic-slice_fusion.3
  282.8 1.0 constant_dynamic-slice_fusion.3
  284.4 1.0 constant_dynamic-slice_fusion.3
  286.0 1.0 constant_dynamic-slice_fusion.3
  287.6 1.0 constant_dynamic-slice_fusion.3
  289.2 1.0 constant_dynamic-slice_fusion.3
  290.8 1.0 constant_dynamic-slice_fusion.3
  292.4 1.0 constant_dynamic-slice_fusion.3
  294.1 1.0 constant_dynamic-slice_fusion.3
  295.7 1.0 constant_dynamic-slice_fusion.3
  297.3 1.0 constant_dynamic-slice_fusion.3
  298.9 1.0 constant_dynamic-slice_fusion.3
  300.5 1.0 constant_dynamic-slice_fusion.3
  302.1 1.0 constant_dynamic-slice_fusion.3
  303.7 1.0 constant_dynamic-slice_fusion.3
  305.3 1.0 constant_dynamic-slice_fusion.3
  306.9 1.0 constant_dynamic-slice_fusion.3
  308.5 1.0 constant_dynamic-slice_fusion.3
  310.1 1.0 constant_dynamic-slice_fusion.3
  311.7 1.0 constant_dynamic-slice_fusion.3
  313.4 1.0 constant_dynamic-slice_fusion.3
  315.0 1.0 constant_dynamic-slice_fusion.3
  316.6 1.0 constant_dynamic-slice_fusion.3
  318.2 1.0 constant_dynamic-slice_fusion.3
  319.8 1.0 constant_dynamic-slice_fusion.3
  321.4 1.0 constant_dynamic-slice_fusion.3
  323.0 0.5 copy.61
  324.2 0.5 subtract_bitcast_fusion
  324.7 1.1 copy-done.1
  325.8 1.1 fusion.27
  327.0 0.6 fusion.18
  327.5 0.6 fusion.16
  328.1 0.8 reshape.255
  (143 shorter events, 24.8 us)
Async XLA Ops:
  6.5 50.6 %all-gather.7.cloned.1.call-start = ((), (), s32[]{:S(2)}) async-start(), calls=%async_computation.1 | async-start | bytes 1474560 | tf_op jit(solution)/shard_map/all_gather | solution.py:77
  10.7 132.8 %all-gather.5.cloned.1.call-start = ((), (), s32[]{:S(2)}) async-start(), calls=%async_computation | async-start | bytes 2211840 | tf_op jit(solution)/shard_map/all_gather | solution.py:64
  11.4 247.3 %all-gather.9.cloned.1.call-start = ((), (), s32[]{:S(2)}) async-start(), calls=%async_computation.2 | async-start | bytes 11796480 | tf_op jit(solution)/shard_map/all_gather | solution.py:85
  143.5 2.8 copy-start
  258.7 65.3 %copy-start.2 = (f32[128]{0:T(128)S(1)}, f32[128]{0:T(128)}, u32[]{:S(2)}) copy-start(f32[128]{0:T(128)} %param.11) | copy-start | bytes 1540
  324.0 1.9 copy-start.1
Sparse Core Ops, SparseCore 0:
  10.8 46.3 all-gather.6
  60.2 83.2 all-gather.4
  145.6 113.0 all-gather.8
where the time goes:
time: 337 us; the launch traced here: 336 us
  waiting for transfers between devices  162 us (48%)
  blocking collectives  75.7 us (22%)
  local copies, waits for them, and re-layouts  53.8 us (16%)
  matrix products  17.7 us (5%)
  between operations  13.2 us (4%)
  other arithmetic  11.7 us (3%)
    all_gather x1, waiting for transfers between devices, shards(): lax.all_gather(level_heads, 'fsdp', axis=0, tiled=True)  107 us
    dynamic_slice x80, local copies, waits for them, and re-layouts, accumulate(): lax.scan(add_block, running, (token_blocks, level_stack, scale_stack))  46.2 us
    all_gather x1, blocking collectives, shards(): lax.all_gather(norm_gain, 'tp', axis=0, tiled=True)  46.1 us
    all_gather x1, waiting for transfers between devices, shards(): lax.all_gather(levels, 'group', axis=3, tiled=True)  45.7 us
    dot_general x40, matrix products, add_block(): jnp.dot(token_rows, level_piece.reshape(BLK, groups_local * head_count *...  16 us
    all_gather x1, blocking collectives, shards(): lax.all_gather(scales, 'group', axis=3, tiled=True)  14.9 us
    all_gather x1, blocking collectives, shards(): lax.all_gather(scale_heads, 'fsdp', axis=0, tiled=True)  14.6 us
    all_gather x1, waiting for transfers between devices, shards(): lax.all_gather(hidden_in, 'tp', axis=2, tiled=True)  8.22 us
  transfers between devices with their start and end apart: 3, of which 3 were waited for; matrix products, arithmetic and copies ran while one was open for 3% of the time, Pallas kernels for 0%

commit v1 on v0

v1 whole, which is shorter than its diff:
```python
import functools

import jax
import jax.numpy as jnp
from jax import lax
from jax.experimental import pallas as pl
from jax.experimental.pallas import tpu as pltpu
from jax.sharding import PartitionSpec as P

MESH = pl.DeviceIdType.MESH
HD = 128
BLK = 128
EPS = 1e-06
ROWS = 48
STEPS = 4
TOK = ROWS * STEPS
KB = 640
HEADS = 8
CACHE = 128
F32 = jnp.float32
BF16 = jnp.bfloat16

ORDER = (0, 7, 1, 6, 2, 5, 3, 4)


def remote(src, dst, send_sem, recv_sem, device):
    return pltpu.make_async_remote_copy(
        src_ref=src,
        dst_ref=dst,
        send_sem=send_sem,
        recv_sem=recv_sem,
        device_id=device,
        device_id_type=MESH,
    )


def kernel(
    hid, ssq, master, gain, lens_row, lens, cache, out,
    wown, wbuf, hbuf, ssqb, psend, pkeep, px, zsend, zkeep, qz, qbuf, cacheb, tcos, tsin, rtok,
    cache_sem, w0_send, w_recv, y_send, h0_send, hx_send, h_recv, s_send, s_recv,
    p_send, p_recv, z_send, z_recv,
):
    g, f, t = lax.axis_index("group"), lax.axis_index("fsdp"), lax.axis_index("tp")
    zl, c = f // 2, f % 2
    zh, x = t // 4, t % 4
    half, pair = zl % 2, zl // 2
    up, down = (lax.rem(g + 1, 8), f, t), (lax.rem(g + 7, 8), f, t)
    right = (g, f, zh * 4 + lax.rem(x + 1, 4))
    left = (g, f, zh * 4 + lax.rem(x + 3, 4))
    other = (g, zl * 2 + (1 - c), t)
    partner = (g, (pair * 2 + (1 - half)) * 2 + c, t)
    is_root = c == x % 2
    hid_f = (pair * 2 + zh) * 2 + x % 2
    root_z = is_root & (zh == half)

    cache_copy = pltpu.make_async_copy(cache, cacheb, cache_sem)
    cache_copy.start()

    bar = pltpu.get_barrier_semaphore()

    def tell(device):
        pl.semaphore_signal(bar, inc=1, device_id=device, device_id_type=MESH)

    for device in (up, down, right, left, other, partner):
        tell(device)
    for k in range(1, 8):
        tell((g, f, lax.rem(t + k, 8)))
    for q in range(2):
        src_z = 2 * half + q

        @pl.when(src_z != zl)
        def _():
            tell((g, src_z * 2 + c, t))

    for tb in range(4):
        src_f = pair * 4 + tb

        @pl.when(is_root & jnp.logical_not((src_f == f) & (zh == half)))
        def _():
            tell((g, src_f, half * 4 + x))

    for blk in range(KB // BLK):
        piece = master[blk * BLK:(blk + 1) * BLK, :]
        largest = jnp.max(jnp.abs(piece))
        scale = (jnp.full((1, HD), largest, F32) + EPS) / 127.0
        scale = scale.astype(BF16).astype(F32)
        level = jnp.floor(piece / scale + 0.5)
        wown[blk * BLK:(blk + 1) * BLK, :] = (level * scale).astype(BF16)

    own_q = zl % 2
    own_used = half == pair

    @pl.when(own_used)
    def _():
        wbuf[0, own_q] = wown[...]

    @pl.when(root_z)
    def _():
        hbuf[x // 2, pl.ds((half * 2 + c) * TOK, TOK), :] = hid[...]

    ssqb[t] = ssq[...]

    n_w = jnp.where(own_used, 1, 2)
    n_h = jnp.where((zl == pair * 2 + zh) & is_root, 1, 2)
    pl.semaphore_wait(bar, 6 + 7 + n_w + n_h)

    def w0_copy(i):
        dst_z = pair + 2 * i
        return dst_z != zl, remote(
            wown, wbuf.at[0, own_q], w0_send.at[i], w_recv.at[0, own_q], (g, dst_z * 2 + c, t)
        )

    def h0_copy(i):
        dst_zh = zh if i == 0 else 1 - zh
        same = (i == 0) & (f == hid_f)
        return jnp.logical_not(same), remote(
            hid,
            hbuf.at[x // 2, pl.ds(((zl % 2) * 2 + c) * TOK, TOK), :],
            h0_send.at[i],
            h_recv.at[x // 2, (zl % 2) * 2 + c],
            (g, hid_f, dst_zh * 4 + x),
        )

    def s_copy(k):
        return remote(ssq, ssqb.at[t], s_send.at[k - 1], s_recv.at[t], (g, f, lax.rem(t + k, 8)))

    def y_copy(direction, k, q):
        if direction == 0:
            src, dst, dev = (8 - k) % 8, 7 - k, up
        else:
            src, dst, dev = k, k + 1, down
        return remote(wbuf.at[src, q], wbuf.at[dst, q], y_send.at[direction, k, q], w_recv.at[dst, q], dev)

    def w_wait(slot, q):
        remote(wbuf.at[slot, q], wbuf.at[slot, q], y_send.at[0, 0, 0], w_recv.at[slot, q], up).wait_recv()

    def h_rows(kb, tb):
        return hbuf.at[kb, pl.ds(tb * TOK, TOK), :]

    def h_wait(kb, tb):
        remote(h_rows(kb, tb), h_rows(kb, tb), hx_send.at[0, 0], h_recv.at[kb, tb], right).wait_recv()

    def hx_copy(kb, tb, direction):
        return remote(
            h_rows(kb, tb), h_rows(kb, tb), hx_send.at[direction, tb], h_recv.at[kb, tb],
            right if direction == 0 else left,
        )

    for i in range(2):
        cond, copy = w0_copy(i)

        @pl.when(cond)
        def _():
            copy.start()

    def start_y(k, q):
        if k < 3 or q == 0:
            y_copy(0, k, q).start()
        if k < 3 or q == 1:
            y_copy(1, k, q).start()

    def first(q):
        @pl.when(2 * half + q != zl)
        def _():
            w_wait(0, q)

        start_y(0, q)

    @pl.when(own_used)
    def _():
        start_y(0, own_q)

    for i in range(2):
        cond, copy = h0_copy(i)

        @pl.when(cond)
        def _():
            copy.start()

    for k in range(1, 8):
        s_copy(k).start()

    kb_root = x // 2
    kb_left = lax.rem(x + 3, 4) // 2
    kb_right = lax.rem(x + 1, 4) // 2

    def h_step(i):
        @pl.when(is_root)
        def _():
            tb = i

            @pl.when(jnp.logical_not(root_z & (half * 2 + c == tb)))
            def _():
                h_wait(kb_root, tb)

            hx_copy(kb_root, tb, 0).start()
            hx_copy(kb_root, tb, 1).start()

        @pl.when(jnp.logical_not(is_root))
        def _():
            if i % 2 == 0:
                tb = i // 2
                h_wait(kb_left, tb)
                hx_copy(kb_left, tb, 0).start()
            else:
                tb = 2 + i // 2
                h_wait(kb_right, tb)
                hx_copy(kb_right, tb, 1).start()

    def first_other(q):
        @pl.when(jnp.logical_not(own_used & (own_q == q)))
        def _():
            w_wait(0, q)
            start_y(0, q)

    def w_step(k, q):
        w_wait(8 - k, q)
        if k < 3 or q == 0:
            y_copy(0, k, q).start()
        w_wait(k, q)
        if k < 3 or q == 1:
            y_copy(1, k, q).start()

    first_other(0)
    first_other(1)

    eye = lax.broadcasted_iota(jnp.int32, (ROWS, ROWS), 0) == lax.broadcasted_iota(jnp.int32, (ROWS, ROWS), 1)
    column = jnp.sum(jnp.where(eye, lens_row[...].astype(F32), 0.0), axis=1, keepdims=True)
    lane = lax.broadcasted_iota(jnp.int32, (1, HD), 1)
    frequency = jnp.exp((lane % 64).astype(F32) * F32(-2.0 / HD * 13.815510557964274))
    sign = jnp.where(lane < 64, -1.0, 1.0).astype(F32)
    gain_row = gain[...] * F32(HD ** -0.5)
    gain_far = pltpu.roll(jnp.broadcast_to(gain_row, (8, HD)), 64, 1)[0:1, :] * sign
    for s in range(STEPS):
        angle = (column + F32(s - STEPS)) * frequency
        tcos[s * ROWS:(s + 1) * ROWS, :] = jnp.cos(angle) * gain_row
        tsin[s * ROWS:(s + 1) * ROWS, :] = jnp.sin(angle) * gain_far

    h_step(0)
    w_step(1, 0)
    h_step(1)
    w_step(1, 1)
    h_step(2)
    w_step(2, 0)
    h_step(3)
    w_step(2, 1)

    for k in range(1, 8):
        tt = lax.rem(t + k, 8)
        remote(ssqb.at[tt], ssqb.at[tt], s_send.at[0], s_recv.at[tt], right).wait_recv()
    total = jnp.sum(ssqb[...], axis=0)
    wide = lax.broadcasted_iota(jnp.int32, (HD, HD), 0) == lax.broadcasted_iota(jnp.int32, (HD, HD), 1)
    col0 = jnp.sum(jnp.where(wide, total[0:1, :], 0.0), axis=1, keepdims=True)
    col1 = jnp.sum(jnp.where(wide, total[1:2, :], 0.0), axis=1, keepdims=True)
    rtok[0:HD, :] = jnp.broadcast_to(lax.rsqrt(col0 * F32(1.0 / 5120) + EPS), (HD, HD))
    rtok[HD:TOK, :] = jnp.broadcast_to(lax.rsqrt(col1 * F32(1.0 / 5120) + EPS), (HD, HD))[0:TOK - HD]

    @pl.when(is_root)
    def _():
        far = lax.rem(x + 2, 4) // 2
        for tb in range(4):
            h_wait(far, tb)

    @pl.when(jnp.logical_not(is_root))
    def _():
        h_wait(kb_left, 2)
        h_wait(kb_left, 3)
        h_wait(kb_right, 0)
        h_wait(kb_right, 1)

    def p_copy(d):
        return remote(psend.at[d], px.at[d], p_send.at[d], p_recv.at[d], other)

    def z_copy(d):
        return remote(zsend.at[d], qz.at[d], z_send.at[d], z_recv.at[d], partner)

    def multiply(d):
        w0 = wbuf[d, 0]
        w1 = wbuf[d, 1]
        for z in range(2):
            for cc in range(2):
                rows = (z * 2 + cc) * TOK
                part = jnp.dot(hbuf[0, rows:rows + TOK, :], w0, preferred_element_type=F32)
                part += jnp.dot(hbuf[1, rows:rows + TOK, :], w1, preferred_element_type=F32)

                @pl.when(c == cc)
                def _():
                    pkeep[d, z] = part

                @pl.when(c != cc)
                def _():
                    psend[d, z] = part.astype(BF16)

        p_copy(d).start()

    def second(d):
        p_copy(d).wait_recv()
        zkeep[d] = pkeep[d, half] + px[d, half].astype(F32)
        zsend[d] = (pkeep[d, 1 - half] + px[d, 1 - half].astype(F32)).astype(BF16)
        z_copy(d).start()

    def third(d):
        z_copy(d).wait_recv()
        head = lax.rem(g + d, 8)
        query = (zkeep[d] + qz[d].astype(F32)) * rtok[...]
        mean = jnp.mean(query * query, axis=1, keepdims=True)
        query = query * lax.rsqrt(mean + EPS)
        turned = query * tcos[...] + pltpu.roll(query, 64, 1) * tsin[...]
        for s in range(STEPS):
            qbuf[pl.ds(head * STEPS + s, ROWS, stride=HEADS * STEPS), :] = turned[s * ROWS:(s + 1) * ROWS, :]

    for i in range(HEADS + 4):
        if i < HEADS:
            d = ORDER[i]
            if i == 3:
                w_step(3, 0)
                w_step(3, 1)
            if d == 4:
                w_wait(4, 0)
                w_wait(4, 1)
            multiply(d)
        if 0 <= i - 2 < HEADS:
            second(ORDER[i - 2])
        if 0 <= i - 4 < HEADS:
            third(ORDER[i - 4])

    cache_copy.wait()
    unroll = 4
    slot = lax.broadcasted_iota(jnp.int32, (HEADS * STEPS, CACHE), 1)
    step = lax.broadcasted_iota(jnp.int32, (HEADS * STEPS, CACHE), 0) % STEPS

    def rows_of(i, carry):
        for u in range(unroll):
            b = i * unroll + u
            query = qbuf[pl.ds(pl.multiple_of(b * HEADS * STEPS, HEADS * STEPS), HEADS * STEPS), :].astype(BF16)
            scores = lax.dot_general(
                query, cacheb[b, :, 0:HD], (((1,), (1,)), ((), ())), preferred_element_type=F32
            )
            scores = jnp.where(slot <= step + (lens[b] - STEPS), scores, -jnp.inf)
            raised = jnp.exp(scores - jnp.max(scores, axis=1, keepdims=True))
            total = jnp.sum(raised, axis=1, keepdims=True)
            result = jnp.dot(raised.astype(BF16), cacheb[b, :, HD:], preferred_element_type=F32)
            out[b] = (result / total).astype(BF16)
        return carry

    lax.fori_loop(0, ROWS // unroll, rows_of, 0)

    for i in range(2):
        for cond, copy in (w0_copy(i), h0_copy(i)):

            @pl.when(cond)
            def _():
                copy.wait_send()

    for k in range(1, 8):
        s_copy(k).wait_send()
    for k in range(4):
        for q in range(2):
            if k < 3 or q == 0:
                y_copy(0, k, q).wait_send()
            if k < 3 or q == 1:
                y_copy(1, k, q).wait_send()
    for tb in range(4):
        @pl.when(is_root)
        def _():
            hx_copy(kb_root, tb, 0).wait_send()
            hx_copy(kb_root, tb, 1).wait_send()

        @pl.when(jnp.logical_not(is_root))
        def _():
            if tb < 2:
                hx_copy(kb_left, tb, 0).wait_send()
            else:
                hx_copy(kb_right, tb, 1).wait_send()
    for d in range(HEADS):
        p_copy(d).wait_send()
        z_copy(d).wait_send()


def shards(hidden_in, norm_gain, master_query, query_gain, kv_cache, lengths):
    floats = hidden_in.astype(F32)
    squares = jnp.sum(floats * floats, axis=-1).T.reshape(1, TOK)
    squares = jnp.pad(squares, ((0, 0), (0, 8 * HD - TOK))).reshape(8, HD)
    gained = (floats * norm_gain.astype(F32)).astype(BF16)
    gained = gained.transpose(1, 0, 2).reshape(TOK, KB)
    vmem = pl.BlockSpec(memory_space=pltpu.VMEM)
    dma = pltpu.SemaphoreType.DMA
    call = pl.pallas_call(
        kernel,
        out_shape=jax.ShapeDtypeStruct((ROWS, HEADS * STEPS, HD), BF16),
        in_specs=[vmem, vmem, vmem, vmem, vmem, pl.BlockSpec(memory_space=pltpu.SMEM), pl.BlockSpec(memory_space=pl.ANY)],
        out_specs=vmem,
        scratch_shapes=[
            pltpu.VMEM((KB, HD), BF16),
            pltpu.VMEM((HEADS, 2, KB, HD), BF16),
            pltpu.VMEM((2, 4 * TOK, KB), BF16),
            pltpu.VMEM((8, 8, HD), F32),
            pltpu.VMEM((HEADS, 2, TOK, HD), BF16),
            pltpu.VMEM((HEADS, 2, TOK, HD), F32),
            pltpu.VMEM((HEADS, 2, TOK, HD), BF16),
            pltpu.VMEM((HEADS, TOK, HD), BF16),
            pltpu.VMEM((HEADS, TOK, HD), F32),
            pltpu.VMEM((HEADS, TOK, HD), BF16),
            pltpu.VMEM((ROWS * HEADS * STEPS, HD), F32),
            pltpu.VMEM((ROWS, CACHE, 2 * HD), BF16),
            pltpu.VMEM((TOK, HD), F32),
            pltpu.VMEM((TOK, HD), F32),
            pltpu.VMEM((TOK, HD), F32),
            dma,
            dma((2,)),
            dma((HEADS, 2)),
            dma((2, 4, 2)),
            dma((2,)),
            dma((2, 4)),
            dma((2, 4)),
            dma((7,)),
            dma((8,)),
            dma((HEADS,)),
            dma((HEADS,)),
            dma((HEADS,)),
            dma((HEADS,)),
        ],
        compiler_params=pltpu.CompilerParams(
            collective_id=0, has_side_effects=True, vmem_limit_bytes=48 << 20
        ),
    )
    result = call(
        gained,
        squares,
        master_query.reshape(KB, HD),
        query_gain.reshape(1, HD),
        lengths.reshape(1, ROWS),
        lengths,
        kv_cache.reshape(ROWS, CACHE, 2 * HD),
    )
    return result.reshape(ROWS, HEADS, STEPS, HD).transpose(0, 2, 1, 3).reshape(ROWS, STEPS, HEADS * HD)


def solution(mesh):
    in_specs = (
        P(("group", "fsdp"), None, "tp"),
        P("tp"),
        P("fsdp", "tp", "group"),
        P(),
        P(("group", "fsdp"), "tp", None, None),
        P(("group", "fsdp")),
    )
    out_specs = P(("group", "fsdp"), None, "tp")
    return jax.shard_map(shards, mesh=mesh, in_specs=in_specs, out_specs=out_specs, check_vma=False)
```

time: 337 us -> 93.3 us (0.28)
  the two profiles are of different devices: /device:TPU:6 before, /device:TPU:1 now
where the time goes in v1:
time: 93.3 us; the launch traced here: 93 us
  Pallas kernels  86 us (92%)
  local copies, waits for them, and re-layouts  5.11 us (5%)
  other arithmetic  1.89 us (2%)
    pallas_call x1, Pallas kernels, shards(): call(gained, squares, master_query.reshape(KB, HD), query_gain.reshape(1,...  86 us
    unnamed x9, local copies, waits for them, and re-layouts  4.91 us

profile of v1, /device:TPU:1, one launch (start us, length us, event | category | flops | bytes accessed | tf_op | source)
XLA Modules:
  0.0 93.0 jit_solution(16236025671069421839)
XLA Ops:
  0.0 0.7 convert_element_type.12
  0.7 1.2 %fusion.1 = (f32[48,4]{1,0:T(8,128)S(1)}, bf16[4,48,640]{2,0,1:T(4,128)(2,1)S(1)}) fusion(bf16[48,4,640]{2,1,0:T(4,128)(2,1)} %param.6, f32[640]{0:T(1024)S(1)} %convert_element_type.12), kind=kLoop, calls=%fused_computation.3 | loop fusion | flops 614208 | bytes 494848 | tf_op jit(solution)/shard_map/reduce_sum | solution.py:382
  1.9 0.1 copy.12
  2.0 0.1 reshape.29
  2.1 0.0 copy-start
  2.1 1.9 %copy-done = bf16[48,1,128,256]{3,2,1,0:T(8,128)(2,1)S(1)} copy-done((bf16[48,1,128,256]{3,2,1,0:T(8,128)(2,1)S(1)}, bf16[48,1,128,256]{3,2,1,0:T(8,128)(2,1)}, u32[]{:S(2)}) %copy-start) | copy-done | bytes 3145752
  4.0 0.0 copy-start.1
  4.0 1.0 %copy-done.1 = f32[640,1,128]{2,1,0:T(1,128)S(1)} copy-done((f32[640,1,128]{2,1,0:T(1,128)S(1)}, f32[640,1,128]{2,1,0:T(1,128)}, u32[]{:S(2)}) %copy-start.1) | copy-done | bytes 327704
  5.0 0.0 copy-start.2
  5.0 0.7 copy-done.2
  5.6 0.0 copy-start.3
  5.6 0.7 copy-done.3
  6.3 86.0 %shard_map.64 = bf16[48,32,128]{2,1,0:T(8,128)(2,1)S(1)} custom-call(bf16[192,640]{1,0:T(8,128)(2,1)S(1)} %bitcast.16, f32[8,128]{1,0:T(8,128)S(1)} %bitcast.18, f32[640,128]{1,0:T(8,128)S(1)} %bitcast.17, f32[1,128]{1,0:T(1,128)S(1)} %bitcast.20, s32[1,48]{1,0:T(1,128)S(1)} %bitcast.19, s32[48]{0:T(128)S(1)} %copy-done.2, bf16[48,128,256]{2,1,0:T(8,128)(2,1)S(1)} %bitcast.14), custom_call_target="tpu_custom_call" | custom-call | tf_op jit(solution)/shard_map/pallas_call | solution.py:427
  92.3 0.7 copy.15
  (2 shorter events, 0.0 us)
Async XLA Ops:
  2.1 1.9 %copy-start = (bf16[48,1,128,256]{3,2,1,0:T(8,128)(2,1)S(1)}, bf16[48,1,128,256]{3,2,1,0:T(8,128)(2,1)}, u32[]{:S(2)}) copy-start(bf16[48,1,128,256]{3,2,1,0:T(8,128)(2,1)} %param.10) | copy-start | bytes 9437188
  4.0 1.0 %copy-start.1 = (f32[640,1,128]{2,1,0:T(1,128)S(1)}, f32[640,1,128]{2,1,0:T(1,128)}, u32[]{:S(2)}) copy-start(f32[640,1,128]{2,1,0:T(1,128)} %param.8) | copy-start | bytes 983044
  5.0 0.7 copy-start.2
  5.6 0.7 copy-start.3

commit v2 on v1

v2 whole, which is shorter than its diff:
```python
import functools

import jax
import jax.numpy as jnp
from jax import lax
from jax.experimental import pallas as pl
from jax.experimental.pallas import tpu as pltpu
from jax.sharding import PartitionSpec as P

MESH = pl.DeviceIdType.MESH
HD = 128
BLK = 128
EPS = 1e-06
ROWS = 48
STEPS = 4
TOK = ROWS * STEPS
KB = 640
HEADS = 8
CACHE = 128
WSUB = 2
WROWS = KB // WSUB
F32 = jnp.float32
BF16 = jnp.bfloat16

GROUPS = ((0,), (7, 1), (6, 2), (5, 3), (4,))


def remote(src, dst, send_sem, recv_sem, device):
    return pltpu.make_async_remote_copy(
        src_ref=src,
        dst_ref=dst,
        send_sem=send_sem,
        recv_sem=recv_sem,
        device_id=device,
        device_id_type=MESH,
    )


def kernel(
    hid_in, gain_in, master_in, qgain_in, lens_in, cache, out,
    hidv, hidf, hid, gain, master, qgain, lens, cacheb,
    wown, wbuf, hbuf, ssqb, psend, pkeep, px, zsend, zkeep, qz, qbuf, tcos, tsin, rtok, last,
    in_sem, w0_send, w_recv, y_send, h0_send, hx_send, h_recv, s_send, s_recv,
    p_send, p_recv, z_send, z_recv,
):
    g, f, t = lax.axis_index("group"), lax.axis_index("fsdp"), lax.axis_index("tp")
    zl, c = f // 2, f % 2
    zh, x = t // 4, t % 4
    side, pair = zl % 2, zl // 2
    half = (side + zh + pair + 1) % 2
    up, down = (lax.rem(g + 1, 8), f, t), (lax.rem(g + 7, 8), f, t)
    right = (g, f, zh * 4 + lax.rem(x + 1, 4))
    left = (g, f, zh * 4 + lax.rem(x + 3, 4))
    other = (g, zl * 2 + (1 - c), t)
    partner = (g, (pair * 2 + (1 - side)) * 2 + c, t)
    is_root = c == x % 2
    root_z = is_root & (zh == half)
    own_tb = side * 2 + c
    own_q = zl % 2
    own_used = half == pair

    inputs = [
        pltpu.make_async_copy(src, dst, in_sem.at[i])
        for i, (src, dst) in enumerate(
            ((master_in, master), (hid_in, hidv), (gain_in, gain), (qgain_in, qgain), (lens_in, lens), (cache, cacheb))
        )
    ]
    for copy in inputs:
        copy.start()

    bar = pltpu.get_barrier_semaphore()

    def tell(device):
        pl.semaphore_signal(bar, inc=1, device_id=device, device_id_type=MESH)

    for q in range(2):
        src_z = 2 * half + q

        @pl.when(src_z != zl)
        def _():
            tell((g, src_z * 2 + c, t))

    for tb in range(4):
        src_f = pair * 4 + tb

        @pl.when(is_root & jnp.logical_not((src_f == f) & (zh == half)))
        def _():
            tell((g, src_f, half * 4 + x))

    for device in (up, down, right, left, other, partner):
        tell(device)
    for k in range(1, 8):
        tell((g, f, lax.rem(t + k, 8)))

    inputs[0].wait()
    for blk in range(KB // BLK):
        piece = master[blk * BLK:(blk + 1) * BLK, :]
        largest = jnp.max(jnp.abs(piece))
        scale = (jnp.full((1, HD), largest, F32) + EPS) / 127.0
        scale = scale.astype(BF16).astype(F32)
        level = jnp.floor(piece / scale + 0.5)
        wown[blk * BLK:(blk + 1) * BLK, :] = (level * scale).astype(BF16)

    @pl.when(own_used)
    def _():
        wbuf[0, own_q] = wown[...]

    n_w = jnp.where(own_used, 1, 2)
    n_h = jnp.where((side != pair) & is_root, 1, 2)
    pl.semaphore_wait(bar, 6 + 7 + n_w + n_h)

    def w0_copy(i, hs):
        dst_z = 2 * i + lax.rem(pair + zh + 1 + i, 2)
        rows = pl.ds(hs * WROWS, WROWS)
        return dst_z != zl, remote(
            wown.at[rows, :], wbuf.at[0, own_q, rows, :], w0_send.at[i, hs], w_recv.at[0, own_q, hs],
            (g, dst_z * 2 + c, t),
        )

    def h0_copy(i, sub):
        dst_side = (1 - pair) if i == 0 else pair
        dst_f = (pair * 2 + dst_side) * 2 + x % 2
        dst_zh = zh if i == 0 else 1 - zh
        needed = jnp.logical_not((side != pair) & is_root) if i == 0 else jnp.bool_(True)
        return needed, remote(
            hid.at[pl.ds(sub * ROWS, ROWS), :],
            hbuf.at[x // 2, sub, pl.ds(own_tb * ROWS, ROWS), :],
            h0_send.at[i, sub],
            h_recv.at[x // 2, own_tb, sub],
            (g, dst_f, dst_zh * 4 + x),
        )

    def s_copy(k):
        return remote(ssqb.at[t], ssqb.at[t], s_send.at[k - 1], s_recv.at[t], (g, f, lax.rem(t + k, 8)))

    def w_rows(slot, q, hs):
        return wbuf.at[slot, q, pl.ds(hs * WROWS, WROWS), :]

    def y_copy(direction, k, q, hs):
        if direction == 0:
            src, dst, dev = (8 - k) % 8, 7 - k, up
        else:
            src, dst, dev = k, k + 1, down
        return remote(
            w_rows(src, q, hs), w_rows(dst, q, hs), y_send.at[direction, k, q, hs], w_recv.at[dst, q, hs], dev
        )

    def w_wait(slot, q, hs):
        rows = w_rows(slot, q, hs)
        remote(rows, rows, y_send.at[0, 0, 0, 0], w_recv.at[slot, q, hs], up).wait_recv()

    def h_rows(kb, tb, sub):
        return hbuf.at[kb, sub, pl.ds(tb * ROWS, ROWS), :]

    def h_wait(kb, tb, sub):
        rows = h_rows(kb, tb, sub)
        remote(rows, rows, hx_send.at[0, 0, 0], h_recv.at[kb, tb, sub], right).wait_recv()

    def hx_copy(kb, tb, sub, direction):
        rows = h_rows(kb, tb, sub)
        return remote(
            rows, rows, hx_send.at[direction, tb, sub], h_recv.at[kb, tb, sub], right if direction == 0 else left
        )

    def start_y(k, q, hs):
        if k < 3 or q == 0:
            y_copy(0, k, q, hs).start()
        if k < 3 or q == 1:
            y_copy(1, k, q, hs).start()

    for i in (1 - pair, pair):
        for hs in range(WSUB):
            cond, copy = w0_copy(i, hs)

            @pl.when(cond)
            def _():
                copy.start()

    @pl.when(own_used)
    def _():
        for hs in range(WSUB):
            start_y(0, own_q, hs)

    inputs[1].wait()
    inputs[2].wait()
    eye = lax.broadcasted_iota(jnp.int32, (ROWS, HD), 0) == lax.broadcasted_iota(jnp.int32, (ROWS, HD), 1)
    for kt in range(KB // HD):
        hidf[kt * TOK:(kt + 1) * TOK, :] = hidv[:, :, kt * HD:(kt + 1) * HD].astype(F32).reshape(TOK, HD)
    gains = gain[...].astype(F32).reshape(1, KB)
    ssq_rows = []
    for s in range(STEPS):
        squares = jnp.zeros((ROWS, HD), F32)
        for kt in range(KB // HD):
            piece = hidf[pl.ds(kt * TOK + s, ROWS, stride=STEPS), :]
            squares += piece * piece
            hid[s * ROWS:(s + 1) * ROWS, kt * HD:(kt + 1) * HD] = (piece * gains[:, kt * HD:(kt + 1) * HD]).astype(BF16)
        ssq_rows.append(
            jnp.sum(jnp.where(eye, jnp.sum(squares, axis=1, keepdims=True), 0.0), axis=0, keepdims=True)
        )
    ssqb[t] = jnp.concatenate(ssq_rows + [jnp.zeros((8 - STEPS, HD), F32)], axis=0)

    for sub in range(STEPS):
        for i in (1, 0):
            cond, copy = h0_copy(i, sub)

            @pl.when(cond)
            def _():
                copy.start()

    for k in range(1, 8):
        s_copy(k).start()

    @pl.when(root_z)
    def _():
        for sub in range(STEPS):
            hbuf[x // 2, sub, pl.ds(own_tb * ROWS, ROWS), :] = hid[sub * ROWS:(sub + 1) * ROWS, :]

    kb_root = x // 2
    kb_left = lax.rem(x + 3, 4) // 2
    kb_right = lax.rem(x + 1, 4) // 2

    def h_step(sub):
        @pl.when(is_root)
        def _():
            for tb in range(4):
                @pl.when(jnp.logical_not(root_z & (own_tb == tb)))
                def _():
                    h_wait(kb_root, tb, sub)

                hx_copy(kb_root, tb, sub, 0).start()
                hx_copy(kb_root, tb, sub, 1).start()

        @pl.when(jnp.logical_not(is_root))
        def _():
            for tb in range(2):
                h_wait(kb_left, tb, sub)
                hx_copy(kb_left, tb, sub, 0).start()
                h_wait(kb_right, tb + 2, sub)
                hx_copy(kb_right, tb + 2, sub, 1).start()

    def h_last(sub):
        @pl.when(is_root)
        def _():
            far = lax.rem(x + 2, 4) // 2
            for tb in range(4):
                h_wait(far, tb, sub)

        @pl.when(jnp.logical_not(is_root))
        def _():
            for tb in range(2):
                h_wait(kb_left, tb + 2, sub)
                h_wait(kb_right, tb, sub)

    def first_other(hs):
        for q in range(2):
            @pl.when(jnp.logical_not(own_used & (own_q == q)))
            def _():
                w_wait(0, q, hs)
                start_y(0, q, hs)

    def w_step(k, q):
        for hs in range(WSUB):
            w_wait(8 - k, q, hs)
            if k < 3 or q == 0:
                y_copy(0, k, q, hs).start()
            w_wait(k, q, hs)
            if k < 3 or q == 1:
                y_copy(1, k, q, hs).start()

    for hs in range(WSUB):
        first_other(hs)

    inputs[3].wait()
    inputs[4].wait()
    lens_row = lens[...].astype(F32).reshape(1, ROWS)
    lens_wide = jnp.concatenate([lens_row, jnp.zeros((1, HD - ROWS), F32)], axis=1)
    column = jnp.sum(jnp.where(eye, lens_wide, 0.0), axis=1, keepdims=True)
    lane = lax.broadcasted_iota(jnp.int32, (1, HD), 1)
    frequency = jnp.exp((lane % 64).astype(F32) * F32(-2.0 / HD * 13.815510557964274))
    sign = jnp.where(lane < 64, -1.0, 1.0).astype(F32)
    gain_row = qgain[...].reshape(1, HD) * F32(HD ** -0.5)
    gain_far = pltpu.roll(jnp.broadcast_to(gain_row, (8, HD)), 64, 1)[0:1, :] * sign
    for s in range(STEPS):
        angle = (column + F32(s - STEPS)) * frequency
        tcos[s * ROWS:(s + 1) * ROWS, :] = jnp.cos(angle) * gain_row
        tsin[s * ROWS:(s + 1) * ROWS, :] = jnp.sin(angle) * gain_far
    row_at = lax.broadcasted_iota(jnp.int32, (ROWS, HD), 0)
    lane_at = lax.broadcasted_iota(jnp.int32, (ROWS, HD), 1)
    for i in range(ROWS // 4):
        chosen = jnp.sum(jnp.where(row_at == 4 * i + lane_at // 32, column, 0.0), axis=0, keepdims=True)
        last[i] = jnp.broadcast_to(chosen + (lane % STEPS - STEPS).astype(F32), (8, HD))

    h_step(0)
    w_step(1, 0)
    h_step(1)
    h_step(2)
    w_step(1, 1)
    h_step(3)
    w_step(2, 0)
    w_step(2, 1)

    for k in range(1, 8):
        tt = lax.rem(t + k, 8)
        remote(ssqb.at[tt], ssqb.at[tt], s_send.at[0], s_recv.at[tt], right).wait_recv()
    total = jnp.sum(ssqb[...], axis=0)
    for s in range(STEPS):
        mean = jnp.sum(jnp.where(eye, total[s:s + 1, :], 0.0), axis=1, keepdims=True) * F32(1.0 / 5120)
        rtok[s * ROWS:(s + 1) * ROWS, :] = jnp.broadcast_to(lax.rsqrt(mean + EPS), (ROWS, HD))

    def p_copy(sub, n):
        lanes = pl.ds(0, HD * len(GROUPS[n]))
        return remote(
            psend.at[sub, n, :, :, lanes], px.at[sub, n, :, :, lanes], p_send.at[sub, n], p_recv.at[sub, n], other
        )

    def z_copy(sub, n):
        lanes = pl.ds(0, HD * len(GROUPS[n]))
        return remote(
            zsend.at[sub, n, :, lanes], qz.at[sub, n, :, lanes], z_send.at[sub, n], z_recv.at[sub, n], partner
        )

    def multiply(sub, n):
        width = HD * len(GROUPS[n])
        weights = jnp.concatenate(
            [jnp.concatenate([wbuf[d, 0], wbuf[d, 1]], axis=0) for d in GROUPS[n]], axis=1
        )
        tokens = jnp.concatenate([hbuf[0, sub], hbuf[1, sub]], axis=1)
        part = jnp.dot(tokens, weights, preferred_element_type=F32)
        for z in range(2):
            for cc in range(2):
                piece = part[(z * 2 + cc) * ROWS:(z * 2 + cc + 1) * ROWS, :]

                @pl.when(c == cc)
                def _():
                    pkeep[sub, n, z, :, 0:width] = piece

                @pl.when(c != cc)
                def _():
                    psend[sub, n, z, :, 0:width] = piece.astype(BF16)

        p_copy(sub, n).start()

    def second(sub, n):
        width = HD * len(GROUPS[n])
        p_copy(sub, n).wait_recv()
        zkeep[sub, n, :, 0:width] = pkeep[sub, n, side, :, 0:width] + px[sub, n, side, :, 0:width].astype(F32)
        zsend[sub, n, :, 0:width] = (
            pkeep[sub, n, 1 - side, :, 0:width] + px[sub, n, 1 - side, :, 0:width].astype(F32)
        ).astype(BF16)
        z_copy(sub, n).start()

    def third(sub, n):
        z_copy(sub, n).wait_recv()
        rows = slice(sub * ROWS, (sub + 1) * ROWS)
        for m, d in enumerate(GROUPS[n]):
            lanes = slice(m * HD, (m + 1) * HD)
            head = lax.rem(g + d, 8)
            query = (zkeep[sub, n, :, lanes] + qz[sub, n, :, lanes].astype(F32)) * rtok[rows, :]
            mean = jnp.mean(query * query, axis=1, keepdims=True)
            query = query * lax.rsqrt(mean + EPS)
            turned = query * tcos[rows, :] + pltpu.roll(query, 64, 1) * tsin[rows, :]
            qbuf[pl.ds(head * STEPS + sub, ROWS, stride=HEADS * STEPS), :] = turned

    def each(stage, sub, ns):
        for n in ns:
            stage(sub, n)

    h_last(0)
    each(multiply, 0, (0, 1, 2))
    w_step(3, 0)
    h_last(1)
    each(multiply, 1, (0, 1, 2))
    each(second, 0, (0, 1, 2))
    w_step(3, 1)
    h_last(2)
    each(multiply, 2, (0, 1, 2, 3))
    each(second, 1, (0, 1, 2))
    each(third, 0, (0, 1, 2))
    multiply(0, 3)
    multiply(1, 3)
    h_last(3)
    each(multiply, 3, (0, 1, 2, 3))
    each(second, 2, (0, 1, 2, 3))
    second(0, 3)
    second(1, 3)
    each(third, 1, (0, 1, 2))
    for hs in range(WSUB):
        w_wait(4, 0, hs)
        w_wait(4, 1, hs)
    for sub in range(STEPS):
        multiply(sub, 4)
    each(second, 3, (0, 1, 2, 3))
    each(third, 2, (0, 1, 2, 3))
    for sub in range(STEPS):
        second(sub, 4)
    third(0, 3)
    third(1, 3)
    each(third, 3, (0, 1, 2, 3))
    for sub in range(STEPS):
        third(sub, 4)

    inputs[5].wait()
    key_at = lax.broadcasted_iota(jnp.int32, (CACHE, HD), 0).astype(F32)
    lane_row = lax.broadcasted_iota(jnp.int32, (CACHE, HD), 1) // 32

    def four_rows(i, carry):
        base = pl.multiple_of(i * 128, 128)
        queries = jnp.transpose(qbuf[pl.ds(base, 128), :]).astype(BF16)
        scores = jnp.zeros((CACHE, HD), F32)
        for r in range(4):
            one = jnp.dot(cacheb[i * 4 + r, :, 0:HD], queries, preferred_element_type=F32)
            scores = one if r == 0 else jnp.where(lane_row == r, one, scores)
        scores = jnp.where(key_at <= last[i, 0:1, :], scores, -jnp.inf)
        raised = jnp.exp(scores - jnp.max(scores, axis=0, keepdims=True))
        weights = raised * (1.0 / jnp.sum(raised, axis=0, keepdims=True))
        weights = jnp.transpose(weights).astype(BF16)
        for r in range(4):
            result = jnp.dot(weights[r * 32:(r + 1) * 32, :], cacheb[i * 4 + r, :, HD:], preferred_element_type=F32)
            out[i * 4 + r] = result.astype(BF16)
        return carry

    lax.fori_loop(0, ROWS // 4, four_rows, 0, unroll=2)

    for i in range(2):
        for hs in range(WSUB):
            cond, copy = w0_copy(i, hs)

            @pl.when(cond)
            def _():
                copy.wait_send()

        for sub in range(STEPS):
            cond, copy = h0_copy(i, sub)

            @pl.when(cond)
            def _():
                copy.wait_send()

    for k in range(1, 8):
        s_copy(k).wait_send()
    for k in range(4):
        for q in range(2):
            for hs in range(WSUB):
                if k < 3 or q == 0:
                    y_copy(0, k, q, hs).wait_send()
                if k < 3 or q == 1:
                    y_copy(1, k, q, hs).wait_send()
    for sub in range(STEPS):
        @pl.when(is_root)
        def _():
            for tb in range(4):
                hx_copy(kb_root, tb, sub, 0).wait_send()
                hx_copy(kb_root, tb, sub, 1).wait_send()

        @pl.when(jnp.logical_not(is_root))
        def _():
            for tb in range(2):
                hx_copy(kb_left, tb, sub, 0).wait_send()
                hx_copy(kb_right, tb + 2, sub, 1).wait_send()

    for sub in range(STEPS):
        for n in range(len(GROUPS)):
            p_copy(sub, n).wait_send()
            z_copy(sub, n).wait_send()


def shards(hidden_in, norm_gain, master_query, query_gain, kv_cache, lengths):
    dma = pltpu.SemaphoreType.DMA
    call = pl.pallas_call(
        kernel,
        out_shape=jax.ShapeDtypeStruct((ROWS, HEADS * STEPS, HD), BF16),
        in_specs=[pl.BlockSpec(memory_space=pltpu.HBM)] * 6,
        out_specs=pl.BlockSpec(memory_space=pltpu.VMEM),
        scratch_shapes=[
            pltpu.VMEM((ROWS, STEPS, KB), BF16),
            pltpu.VMEM((KB // HD * TOK, HD), F32),
            pltpu.VMEM((TOK, KB), BF16),
            pltpu.VMEM((KB,), BF16),
            pltpu.VMEM((KB, HD), F32),
            pltpu.VMEM((HD,), F32),
            pltpu.VMEM((ROWS,), jnp.int32),
            pltpu.VMEM((ROWS, CACHE, 2 * HD), BF16),
            pltpu.VMEM((KB, HD), BF16),
            pltpu.VMEM((HEADS, 2, KB, HD), BF16),
            pltpu.VMEM((2, STEPS, 4 * ROWS, KB), BF16),
            pltpu.VMEM((8, 8, HD), F32),
            pltpu.VMEM((STEPS, len(GROUPS), 2, ROWS, 2 * HD), BF16),
            pltpu.VMEM((STEPS, len(GROUPS), 2, ROWS, 2 * HD), F32),
            pltpu.VMEM((STEPS, len(GROUPS), 2, ROWS, 2 * HD), BF16),
            pltpu.VMEM((STEPS, len(GROUPS), ROWS, 2 * HD), BF16),
            pltpu.VMEM((STEPS, len(GROUPS), ROWS, 2 * HD), F32),
            pltpu.VMEM((STEPS, len(GROUPS), ROWS, 2 * HD), BF16),
            pltpu.VMEM((ROWS * HEADS * STEPS, HD), F32),
            pltpu.VMEM((TOK, HD), F32),
            pltpu.VMEM((TOK, HD), F32),
            pltpu.VMEM((TOK, HD), F32),
            pltpu.VMEM((ROWS // 4, 8, HD), F32),
            dma((6,)),
            dma((2, WSUB)),
            dma((HEADS, 2, WSUB)),
            dma((2, 4, 2, WSUB)),
            dma((2, STEPS)),
            dma((2, 4, STEPS)),
            dma((2, 4, STEPS)),
            dma((7,)),
            dma((8,)),
            dma((STEPS, len(GROUPS))),
            dma((STEPS, len(GROUPS))),
            dma((STEPS, len(GROUPS))),
            dma((STEPS, len(GROUPS))),
        ],
        compiler_params=pltpu.CompilerParams(
            collective_id=0, has_side_effects=True, vmem_limit_bytes=62 << 20
        ),
    )
    result = call(
        hidden_in,
        norm_gain,
        master_query.reshape(KB, HD),
        query_gain,
        lengths,
        kv_cache.reshape(ROWS, CACHE, 2 * HD),
    )
    return result.reshape(ROWS, HEADS, STEPS, HD).transpose(0, 2, 1, 3).reshape(ROWS, STEPS, HEADS * HD)


def solution(mesh):
    in_specs = (
        P(("group", "fsdp"), None, "tp"),
        P("tp"),
        P("fsdp", "tp", "group"),
        P(),
        P(("group", "fsdp"), "tp", None, None),
        P(("group", "fsdp")),
    )
    out_specs = P(("group", "fsdp"), None, "tp")
    return jax.shard_map(shards, mesh=mesh, in_specs=in_specs, out_specs=out_specs, check_vma=False)
```

time: 93.3 us -> 78.1 us (0.84)
  the two profiles are of different devices: /device:TPU:1 before, /device:TPU:6 now
where the time goes in v2:
time: 78.1 us; the launch traced here: 78 us
  Pallas kernels  76.1 us (97%)
  local copies, waits for them, and re-layouts  1.88 us (2%)
    pallas_call x1, Pallas kernels, shards(): call(hidden_in, norm_gain, master_query.reshape(KB, HD), query_gain, leng...  76.1 us
    unnamed x1, local copies, waits for them, and re-layouts  1.88 us

profile of v2, /device:TPU:6, one launch (start us, length us, event | category | flops | bytes accessed | tf_op | source)
XLA Modules:
  0.0 78.0 jit_solution(16617454819098391864)
XLA Ops:
  0.0 76.1 %shard_map.64 = bf16[48,32,128]{2,1,0:T(8,128)(2,1)} custom-call(bf16[48,4,640]{2,1,0:T(4,128)(2,1)} %hid_in.1, bf16[640]{0:T(1024)(128)(2,1)} %gain_in.1, f32[640,128]{1,0:T(8,128)} %bitcast.9, f32[128]{0:T(128)} %qgain_in.1, s32[48]{0:T(128)} %lens_in.1, bf16[48,128,256]{2,1,0:T(8,128)(2,1)} %bitcast.7), custom_call_target="tpu_custom_call" | custom-call | tf_op jit(solution)/shard_map/pallas_call | solution.py:516
  76.1 1.9 %copy.9 = bf16[48,4,1024]{2,1,0:T(4,128)(2,1)} copy(bf16[48,4,1024]{2,1,0:T(4,128)(2,1)} %bitcast.8) | data formatting | bytes 786432

commit v3 on v2

v3 whole, which is shorter than its diff:
```python
import functools

import jax
import jax.numpy as jnp
from jax import lax
from jax.experimental import pallas as pl
from jax.experimental.pallas import tpu as pltpu
from jax.sharding import PartitionSpec as P

MESH = pl.DeviceIdType.MESH
HD = 128
BLK = 128
EPS = 1e-06
ROWS = 48
STEPS = 4
TOK = ROWS * STEPS
KB = 640
HEADS = 8
CACHE = 128
SUBS = 4
LATE = 2
SUB = TOK // SUBS
PIECES = ((0, 3), (6, 2), (3, 3), (8, 2))
F32 = jnp.float32
BF16 = jnp.bfloat16

GROUPS = ((0, 7, 1), (6, 2), (5, 3))
WIDE = 3 * HD


def remote(src, dst, send_sem, recv_sem, device):
    return pltpu.make_async_remote_copy(
        src_ref=src,
        dst_ref=dst,
        send_sem=send_sem,
        recv_sem=recv_sem,
        device_id=device,
        device_id_type=MESH,
    )


def kernel(
    hid_in, gain_in, master_in, qgain_in, lens_in, cache, out,
    hidv, hidf, hid, gain, master, qgain, lens, cacheb,
    wown, wbuf, hbuf, ssqb, psend, pkeep, px, zsend, zkeep, qz,
    psend4, pkeep4, px4, zsend4, zkeep4, qz4, qbuf, tcos, tsin, rtok, last,
    in_sem, w0_send, w_recv, y_send, h0_send, hx_send, hz_recv, hx_recv, s_send, s_recv,
    p_send, p_recv, z_send, z_recv, last_sem,
):
    g, f, t = lax.axis_index("group"), lax.axis_index("fsdp"), lax.axis_index("tp")
    zl, c = f // 2, f % 2
    zh, x = t // 4, t % 4
    side, pair = zl % 2, zl // 2
    up, down = (lax.rem(g + 1, 8), f, t), (lax.rem(g + 7, 8), f, t)
    right = (g, f, zh * 4 + lax.rem(x + 1, 4))
    left = (g, f, zh * 4 + lax.rem(x + 3, 4))
    other = (g, zl * 2 + (1 - c), t)
    partner = (g, (pair * 2 + (1 - side)) * 2 + c, t)
    is_root = c == x % 2
    own_tb = side * 2 + c
    inputs = [
        pltpu.make_async_copy(src, dst, in_sem.at[i])
        for i, (src, dst) in enumerate(
            ((master_in, master), (hid_in, hidv), (gain_in, gain), (qgain_in, qgain), (lens_in, lens), (cache, cacheb))
        )
    ]
    for copy in inputs:
        copy.start()

    def z_at(k):
        k_pair, k_side = k // 2, k % 2
        return (g, (lax.rem(pair + k_pair, 2) * 2 + lax.rem(side + k_side, 2)) * 2 + c, t)

    bar = pltpu.get_barrier_semaphore()

    def tell(device):
        pl.semaphore_signal(bar, inc=1, device_id=device, device_id_type=MESH)

    for k in range(1, 4):
        tell(z_at(k))

    for src_zh in range(2):
        for tb in range(4):
            src_f = pair * 4 + tb

            @pl.when(is_root & jnp.logical_not((src_f == f) & (zh == src_zh)))
            def _():
                tell((g, src_f, src_zh * 4 + x))

    for device in (up, down, right, left, other, partner):
        tell(device)
    for k in range(1, 8):
        tell((g, f, lax.rem(t + k, 8)))

    inputs[0].wait()
    for blk in range(KB // BLK):
        piece = master[blk * BLK:(blk + 1) * BLK, :]
        largest = jnp.max(jnp.abs(piece), axis=(0, 1), keepdims=True)
        scale = (largest + EPS) / 127.0
        scale = scale.astype(BF16).astype(F32)
        level = jnp.floor(piece / scale + 0.5)
        wown[blk * BLK:(blk + 1) * BLK, :] = (level * scale).astype(BF16)

    wbuf[0, 0:3 * HD, :] = wown[0:3 * HD, :]

    pl.semaphore_wait(bar, 3 + 6 + 7 + jnp.where(is_root, 3, 4))

    def w0_copy(k):
        first, tiles = PIECES[k]
        start = 0 if tiles == 3 else 3
        return remote(
            wown.at[pl.ds(start * HD, tiles * HD), :], w_rows(0, k), w0_send.at[k - 1], w_recv.at[0, k], z_at(k)
        )

    def h0_copy(match, plane, sub):
        tiles, start = (3, 0) if match == 0 else (2, 3)
        dst_side = lax.rem(x // 2 + match, 2)
        dst_f = (pair * 2 + dst_side) * 2 + x % 2
        rel = lax.rem(zh + pair, 2)
        same = is_root & (side == dst_side) if plane == 0 else jnp.bool_(False)
        first = rel * tiles + (0 if match == 0 else 6)
        return jnp.logical_not(same), first, remote(
            hid.at[pl.ds(start, tiles), pl.ds(sub * SUB, SUB), :],
            hbuf.at[pl.ds(first, tiles), sub, pl.ds(own_tb * SUB, SUB), :],
            h0_send.at[match, plane, sub],
            hz_recv.at[rel, own_tb, sub],
            (g, dst_f, (zh if plane == 0 else 1 - zh) * 4 + x),
        )

    def s_copy(k):
        return remote(ssqb.at[t], ssqb.at[t], s_send.at[k - 1], s_recv.at[t], (g, f, lax.rem(t + k, 8)))

    def w_rows(slot, p):
        first, tiles = PIECES[p]
        return wbuf.at[slot, pl.ds(first * HD, tiles * HD), :]

    def y_copy(direction, k, p):
        if direction == 0:
            src, dst, dev = (8 - k) % 8, 7 - k, up
        else:
            src, dst, dev = k, k + 1, down
        return remote(w_rows(src, p), w_rows(dst, p), y_send.at[direction, k, p], w_recv.at[dst, p], dev)

    def y_goes(direction, k, p):
        return k < 3 or p // 2 == direction

    def w_wait(slot, p):
        rows = w_rows(slot, p)
        remote(rows, rows, y_send.at[0, 0, 0], w_recv.at[slot, p], up).wait_recv()

    def hz_wait(match, rel, tb, sub):
        tiles = 3 if match == 0 else 2
        rows = hbuf.at[pl.ds((0 if match == 0 else 6) + rel * tiles, tiles), sub, pl.ds(tb * SUB, SUB), :]
        remote(rows, rows, hx_send.at[0, 0, 0], hz_recv.at[rel, tb, sub], right).wait_recv()

    def h_rows(match, tp, sub):
        tiles = pl.ds(0, 6) if match == 0 else pl.ds(6, 4)
        return hbuf.at[tiles, sub, pl.ds(tp * 2 * SUB, 2 * SUB), :]

    def h_wait(match, tp, sub):
        rows = h_rows(match, tp, sub)
        remote(rows, rows, hx_send.at[0, 0, 0], hx_recv.at[match, tp, sub], right).wait_recv()

    def hx_copy(match, tp, sub, direction):
        rows = h_rows(match, tp, sub)
        return remote(
            rows, rows, hx_send.at[direction, tp, sub], hx_recv.at[match, tp, sub],
            right if direction == 0 else left,
        )

    def start_y(k, p):
        for direction in range(2):
            if y_goes(direction, k, p):
                y_copy(direction, k, p).start()

    start_y(0, 0)
    w0_copy(1).start()

    inputs[1].wait()
    inputs[2].wait()
    eye = lax.broadcasted_iota(jnp.int32, (ROWS, HD), 0) == lax.broadcasted_iota(jnp.int32, (ROWS, HD), 1)
    for kt in range(KB // HD):
        hidf[kt * TOK:(kt + 1) * TOK, :] = hidv[:, :, kt * HD:(kt + 1) * HD].astype(F32).reshape(TOK, HD)
    gains = gain[...].astype(F32).reshape(1, KB)
    ssq_rows = []
    for s in range(STEPS):
        squares = jnp.zeros((ROWS, HD), F32)
        for kt in range(KB // HD):
            piece = hidf[pl.ds(kt * TOK + s, ROWS, stride=STEPS), :]
            squares += piece * piece
            hid[kt, s * ROWS:(s + 1) * ROWS, :] = (piece * gains[:, kt * HD:(kt + 1) * HD]).astype(BF16)
        ssq_rows.append(
            jnp.sum(jnp.where(eye, jnp.sum(squares, axis=1, keepdims=True), 0.0), axis=0, keepdims=True)
        )
    ssqb[t] = jnp.concatenate(ssq_rows + [jnp.zeros((8 - STEPS, HD), F32)], axis=0)

    for sub in range(SUBS):
        if sub == LATE:
            w0_copy(2).start()
            w0_copy(3).start()
        for plane in (1, 0):
            for match in range(2):
                cond, first, copy = h0_copy(match, plane, sub)

                @pl.when(cond)
                def _():
                    copy.start()

    if LATE == SUBS:
        w0_copy(2).start()
        w0_copy(3).start()
    for k in range(1, 8):
        s_copy(k).start()

    rel_own = lax.rem(zh + pair, 2)
    for match in range(2):
        tiles, start = (3, 0) if match == 0 else (2, 3)

        @pl.when(is_root & (side == lax.rem(x // 2 + match, 2)))
        def _():
            for sub in range(SUBS):
                for kt in range(tiles):
                    hbuf[rel_own * tiles + (0 if match == 0 else 6) + kt, sub, pl.ds(own_tb * SUB, SUB), :] = hid[
                        start + kt, sub * SUB:(sub + 1) * SUB, :
                    ]

    root_match = x // 2 == side
    left_match = lax.rem(x + 3, 4) // 2 == side

    def for_match(flag, body):
        @pl.when(flag)
        def _():
            body(0)

        @pl.when(jnp.logical_not(flag))
        def _():
            body(1)

    def h_step(sub):
        @pl.when(is_root)
        def _():
            def root(match):
                for tp in range(2):
                    for tb in (2 * tp, 2 * tp + 1):
                        for rel in range(2):
                            @pl.when(jnp.logical_not((rel_own == rel) & (own_tb == tb)))
                            def _():
                                hz_wait(match, rel, tb, sub)

                    hx_copy(match, tp, sub, 0).start()
                    hx_copy(match, tp, sub, 1).start()

            for_match(root_match, root)

        @pl.when(jnp.logical_not(is_root))
        def _():
            def passer(match):
                h_wait(match, 0, sub)
                hx_copy(match, 0, sub, 0).start()
                h_wait(1 - match, 1, sub)
                hx_copy(1 - match, 1, sub, 1).start()

            for_match(left_match, passer)

    def h_last(sub):
        @pl.when(is_root)
        def _():
            def root(match):
                for tp in range(2):
                    h_wait(1 - match, tp, sub)

            for_match(root_match, root)

        @pl.when(jnp.logical_not(is_root))
        def _():
            def passer(match):
                h_wait(match, 1, sub)
                h_wait(1 - match, 0, sub)

            for_match(left_match, passer)

    def w_step(k, p):
        w_wait(8 - k, p)
        if y_goes(0, k, p):
            y_copy(0, k, p).start()
        w_wait(k, p)
        if y_goes(1, k, p):
            y_copy(1, k, p).start()

    def w_first(p):
        w_wait(0, p)
        start_y(0, p)

    w_first(1)

    inputs[3].wait()
    inputs[4].wait()
    lens_row = lens[...].astype(F32).reshape(1, ROWS)
    lens_wide = jnp.concatenate([lens_row, jnp.zeros((1, HD - ROWS), F32)], axis=1)
    column = jnp.sum(jnp.where(eye, lens_wide, 0.0), axis=1, keepdims=True)
    lane = lax.broadcasted_iota(jnp.int32, (1, HD), 1)
    frequency = jnp.exp((lane % 64).astype(F32) * F32(-2.0 / HD * 13.815510557964274))
    sign = jnp.where(lane < 64, -1.0, 1.0).astype(F32)
    gain_row = qgain[...].reshape(1, HD) * F32(HD ** -0.5)
    gain_far = pltpu.roll(jnp.broadcast_to(gain_row, (8, HD)), 64, 1)[0:1, :] * sign
    for s in range(STEPS):
        angle = (column + F32(s - STEPS)) * frequency
        tcos[s * ROWS:(s + 1) * ROWS, :] = jnp.cos(angle) * gain_row
        tsin[s * ROWS:(s + 1) * ROWS, :] = jnp.sin(angle) * gain_far
    row_at = lax.broadcasted_iota(jnp.int32, (ROWS, HD), 0)
    lane_at = lax.broadcasted_iota(jnp.int32, (ROWS, HD), 1)
    for i in range(ROWS // 4):
        chosen = jnp.sum(jnp.where(row_at == 4 * i + lane_at // 32, column, 0.0), axis=0, keepdims=True)
        last[i] = jnp.broadcast_to(chosen + (lane % STEPS - STEPS).astype(F32), (8, HD))

    w_step(1, 0)
    w_step(1, 1)
    h_step(0)
    w_step(2, 0)
    w_step(2, 1)
    h_step(1)
    w_first(2)
    w_first(3)
    w_step(3, 0)
    w_step(3, 1)
    h_step(2)
    w_step(1, 2)
    w_step(1, 3)
    h_step(3)

    for k in range(1, 8):
        tt = lax.rem(t + k, 8)
        remote(ssqb.at[tt], ssqb.at[tt], s_send.at[0], s_recv.at[tt], right).wait_recv()
    total = jnp.sum(ssqb[...], axis=0)
    for s in range(STEPS):
        mean = jnp.sum(jnp.where(eye, total[s:s + 1, :], 0.0), axis=1, keepdims=True) * F32(1.0 / 5120)
        rtok[s * ROWS:(s + 1) * ROWS, :] = jnp.broadcast_to(lax.rsqrt(mean + EPS), (ROWS, HD))

    def p_copy(u, n):
        lanes = pl.ds(0, HD * len(GROUPS[n]))
        return remote(
            psend.at[u, n, :, :, lanes], px.at[u, n, :, :, lanes], p_send.at[u, n], p_recv.at[u, n], other
        )

    def z_copy(u, n):
        lanes = pl.ds(0, HD * len(GROUPS[n]))
        return remote(
            zsend.at[u, n, :, lanes], qz.at[u, n, :, lanes], z_send.at[u, n], z_recv.at[u, n], partner
        )

    def tokens_of(subs):
        return jnp.concatenate(
            [jnp.concatenate([hbuf[kt, sub] for kt in range(2 * KB // HD)], axis=1) for sub in subs], axis=0
        )

    def subs_of(u):
        return range(u * SUBS // 2, (u + 1) * SUBS // 2)

    def split(part, m, z):
        first_core = part[(m * 4 + z * 2) * SUB:(m * 4 + z * 2 + 1) * SUB, :]
        second_core = part[(m * 4 + z * 2 + 1) * SUB:(m * 4 + z * 2 + 2) * SUB, :]
        return jnp.where(c == 0, first_core, second_core), jnp.where(c == 0, second_core, first_core).astype(BF16)

    def multiply(u, n):
        width = HD * len(GROUPS[n])
        weights = jnp.concatenate([wbuf[d] for d in GROUPS[n]], axis=1)
        part = jnp.dot(tokens_of(subs_of(u)), weights, preferred_element_type=F32)
        for m in range(SUBS // 2):
            for z in range(2):
                keep, send = split(part, m, z)
                pkeep[u, n, z, m * SUB:(m + 1) * SUB, 0:width] = keep
                psend[u, n, z, m * SUB:(m + 1) * SUB, 0:width] = send
        p_copy(u, n).start()

    def second(u, n):
        width = HD * len(GROUPS[n])
        p_copy(u, n).wait_recv()
        zkeep[u, n, :, 0:width] = pkeep[u, n, side, :, 0:width] + px[u, n, side, :, 0:width].astype(F32)
        zsend[u, n, :, 0:width] = (
            pkeep[u, n, 1 - side, :, 0:width] + px[u, n, 1 - side, :, 0:width].astype(F32)
        ).astype(BF16)
        z_copy(u, n).start()

    def finish(queries, rows):
        means = [jnp.mean(query * query, axis=1, keepdims=True) for query in queries]
        queries = [query * lax.rsqrt(mean + EPS) for query, mean in zip(queries, means)]
        cosines, sines = tcos[rows, :], tsin[rows, :]
        return [query * cosines + pltpu.roll(query, 64, 1) * sines for query in queries]

    def third(u):
        rows = slice(u * 2 * ROWS, (u + 1) * 2 * ROWS)
        slots, queries = [], []
        for n in range(len(GROUPS)):
            z_copy(u, n).wait_recv()
        factors = rtok[rows, :]
        for n in range(len(GROUPS)):
            for m, d in enumerate(GROUPS[n]):
                lanes = slice(m * HD, (m + 1) * HD)
                slots.append(d)
                queries.append((zkeep[u, n, :, lanes] + qz[u, n, :, lanes].astype(F32)) * factors)
        for d, turned in zip(slots, finish(queries, rows)):
            head = lax.rem(g + d, 8)
            for m in range(2):
                qbuf[pl.ds(head * STEPS + 2 * u + m, ROWS, stride=HEADS * STEPS), :] = turned[m * ROWS:(m + 1) * ROWS, :]

    def p4_copy():
        return remote(psend4, px4, last_sem.at[0], last_sem.at[1], other)

    def z4_copy():
        return remote(zsend4, qz4, last_sem.at[2], last_sem.at[3], partner)

    def multiply4():
        part = jnp.dot(tokens_of(range(SUBS)), wbuf[4], preferred_element_type=F32)
        for sub in range(SUBS):
            rows = slice(sub * SUB, (sub + 1) * SUB)
            for z in range(2):
                pkeep4[z, rows, :], psend4[z, rows, :] = split(part, sub, z)
        p4_copy().start()

    def second4():
        p4_copy().wait_recv()
        zkeep4[...] = pkeep4[side] + px4[side].astype(F32)
        zsend4[...] = (pkeep4[1 - side] + px4[1 - side].astype(F32)).astype(BF16)
        z4_copy().start()

    def third4():
        z4_copy().wait_recv()
        head = lax.rem(g + 4, 8)
        query = (zkeep4[...] + qz4[...].astype(F32)) * rtok[...]
        turned = finish([query], slice(0, TOK))[0]
        for sub in range(STEPS):
            qbuf[pl.ds(head * STEPS + sub, ROWS, stride=HEADS * STEPS), :] = turned[sub * ROWS:(sub + 1) * ROWS, :]

    def early_sent():
        for k in (1, 2, 3):
            w0_copy(k).wait_send()
        for sub in range(SUBS):
            for plane in range(2):
                for match in range(2):
                    cond, first, copy = h0_copy(match, plane, sub)

                    @pl.when(cond)
                    def _():
                        copy.wait_send()

        for k in range(1, 8):
            s_copy(k).wait_send()
        for k in range(3):
            for p in range(4):
                y_copy(0, k, p).wait_send()
                y_copy(1, k, p).wait_send()
        for sub in range(SUBS):
            @pl.when(is_root)
            def _():
                def root(match):
                    for tp in range(2):
                        hx_copy(match, tp, sub, 0).wait_send()
                        hx_copy(match, tp, sub, 1).wait_send()

                for_match(root_match, root)

            @pl.when(jnp.logical_not(is_root))
            def _():
                def passer(match):
                    hx_copy(match, 0, sub, 0).wait_send()
                    hx_copy(1 - match, 1, sub, 1).wait_send()

                for_match(left_match, passer)

    h_last(0)
    w_step(2, 2)
    w_step(2, 3)
    h_last(1)
    multiply(0, 0)
    multiply(0, 1)
    w_step(3, 2)
    w_step(3, 3)
    second(0, 0)
    second(0, 1)
    h_last(2)
    multiply(0, 2)
    h_last(3)
    multiply(1, 0)
    multiply(1, 1)
    multiply(1, 2)
    second(0, 2)
    early_sent()
    for p in range(4):
        w_wait(4, p)
    multiply4()
    second(1, 0)
    second(1, 1)
    second(1, 2)
    second4()
    third(0)
    third(1)
    third4()

    inputs[5].wait()
    key_at = lax.broadcasted_iota(jnp.int32, (CACHE, HD), 0).astype(F32)
    lane_row = lax.broadcasted_iota(jnp.int32, (CACHE, HD), 1) // 32

    def four_rows(i, carry):
        base = pl.multiple_of(i * 128, 128)
        queries = jnp.transpose(qbuf[pl.ds(base, 128), :]).astype(BF16)
        scores = jnp.zeros((CACHE, HD), F32)
        for r in range(4):
            one = jnp.dot(cacheb[i * 4 + r, :, 0:HD], queries, preferred_element_type=F32)
            scores = one if r == 0 else jnp.where(lane_row == r, one, scores)
        scores = jnp.where(key_at <= last[i, 0:1, :], scores, -jnp.inf)
        raised = jnp.exp(scores - jnp.max(scores, axis=0, keepdims=True))
        weights = raised * (1.0 / jnp.sum(raised, axis=0, keepdims=True))
        weights = jnp.transpose(weights).astype(BF16)
        for r in range(4):
            result = jnp.dot(weights[r * 32:(r + 1) * 32, :], cacheb[i * 4 + r, :, HD:], preferred_element_type=F32)
            out[i * 4 + r] = result.astype(BF16)
        return carry

    lax.fori_loop(0, ROWS // 4, four_rows, 0, unroll=6)

    for p in range(4):
        y_copy(p // 2, 3, p).wait_send()
    for u in range(2):
        for n in range(len(GROUPS)):
            p_copy(u, n).wait_send()
            z_copy(u, n).wait_send()
    p4_copy().wait_send()
    z4_copy().wait_send()


def shards(hidden_in, norm_gain, master_query, query_gain, kv_cache, lengths):
    dma = pltpu.SemaphoreType.DMA
    call = pl.pallas_call(
        kernel,
        out_shape=jax.ShapeDtypeStruct((ROWS, HEADS * STEPS, HD), BF16),
        in_specs=[pl.BlockSpec(memory_space=pltpu.HBM)] * 6,
        out_specs=pl.BlockSpec(memory_space=pltpu.VMEM),
        scratch_shapes=[
            pltpu.VMEM((ROWS, STEPS, KB), BF16),
            pltpu.VMEM((KB // HD * TOK, HD), F32),
            pltpu.VMEM((KB // HD, TOK, HD), BF16),
            pltpu.VMEM((KB,), BF16),
            pltpu.VMEM((KB, HD), F32),
            pltpu.VMEM((HD,), F32),
            pltpu.VMEM((ROWS,), jnp.int32),
            pltpu.VMEM((ROWS, CACHE, 2 * HD), BF16),
            pltpu.VMEM((KB, HD), BF16),
            pltpu.VMEM((HEADS, 2 * KB, HD), BF16),
            pltpu.VMEM((2 * KB // HD, SUBS, 4 * SUB, HD), BF16),
            pltpu.VMEM((8, 8, HD), F32),
            pltpu.VMEM((2, len(GROUPS), 2, 2 * ROWS, WIDE), BF16),
            pltpu.VMEM((2, len(GROUPS), 2, 2 * ROWS, WIDE), F32),
            pltpu.VMEM((2, len(GROUPS), 2, 2 * ROWS, WIDE), BF16),
            pltpu.VMEM((2, len(GROUPS), 2 * ROWS, WIDE), BF16),
            pltpu.VMEM((2, len(GROUPS), 2 * ROWS, WIDE), F32),
            pltpu.VMEM((2, len(GROUPS), 2 * ROWS, WIDE), BF16),
            pltpu.VMEM((2, TOK, HD), BF16),
            pltpu.VMEM((2, TOK, HD), F32),
            pltpu.VMEM((2, TOK, HD), BF16),
            pltpu.VMEM((TOK, HD), BF16),
            pltpu.VMEM((TOK, HD), F32),
            pltpu.VMEM((TOK, HD), BF16),
            pltpu.VMEM((ROWS * HEADS * STEPS, HD), F32),
            pltpu.VMEM((TOK, HD), F32),
            pltpu.VMEM((TOK, HD), F32),
            pltpu.VMEM((TOK, HD), F32),
            pltpu.VMEM((ROWS // 4, 8, HD), F32),
            dma((6,)),
            dma((3,)),
            dma((HEADS, 4)),
            dma((2, 4, 4)),
            dma((2, 2, SUBS)),
            dma((2, 2, SUBS)),
            dma((2, 4, SUBS)),
            dma((2, 2, SUBS)),
            dma((7,)),
            dma((8,)),
            dma((2, len(GROUPS))),
            dma((2, len(GROUPS))),
            dma((2, len(GROUPS))),
            dma((2, len(GROUPS))),
            dma((4,)),
        ],
        compiler_params=pltpu.CompilerParams(
            collective_id=0, has_side_effects=True, vmem_limit_bytes=62 << 20
        ),
    )
    result = call(
        hidden_in,
        norm_gain,
        master_query.reshape(KB, HD),
        query_gain,
        lengths,
        kv_cache.reshape(ROWS, CACHE, 2 * HD),
    )
    return result.reshape(ROWS, HEADS, STEPS, HD).transpose(0, 2, 1, 3).reshape(ROWS, STEPS, HEADS * HD)


def solution(mesh):
    in_specs = (
        P(("group", "fsdp"), None, "tp"),
        P("tp"),
        P("fsdp", "tp", "group"),
        P(),
        P(("group", "fsdp"), "tp", None, None),
        P(("group", "fsdp")),
    )
    out_specs = P(("group", "fsdp"), None, "tp")
    return jax.shard_map(shards, mesh=mesh, in_specs=in_specs, out_specs=out_specs, check_vma=False)
```

time: 78.1 us -> 71.2 us (0.912)
  the two profiles are of different devices: /device:TPU:6 before, /device:TPU:2 now
where the time goes in v3:
time: 71.2 us; the launch traced here: 71.1 us
  Pallas kernels  69.2 us (97%)
  local copies, waits for them, and re-layouts  1.88 us (3%)
    pallas_call x1, Pallas kernels, shards(): call(hidden_in, norm_gain, master_query.reshape(KB, HD), query_gain, leng...  69.2 us
    unnamed x1, local copies, waits for them, and re-layouts  1.88 us

profile of v3, /device:TPU:2, one launch (start us, length us, event | category | flops | bytes accessed | tf_op | source)
XLA Modules:
  0.0 71.1 jit_solution(14368274184899876149)
XLA Ops:
  0.0 69.2 %shard_map.64 = bf16[48,32,128]{2,1,0:T(8,128)(2,1)} custom-call(bf16[48,4,640]{2,1,0:T(4,128)(2,1)} %hid_in.1, bf16[640]{0:T(1024)(128)(2,1)} %gain_in.1, f32[640,128]{1,0:T(8,128)} %bitcast.9, f32[128]{0:T(128)} %qgain_in.1, s32[48]{0:T(128)} %lens_in.1, bf16[48,128,256]{2,1,0:T(8,128)(2,1)} %bitcast.7), custom_call_target="tpu_custom_call" | custom-call | tf_op jit(solution)/shard_map/pallas_call | solution.py:588
  69.2 1.9 %copy.9 = bf16[48,4,1024]{2,1,0:T(4,128)(2,1)} copy(bf16[48,4,1024]{2,1,0:T(4,128)(2,1)} %bitcast.8) | data formatting | bytes 786432

commit v4 on v3

--- a/solution.py
+++ b/solution.py
@@ -103,79 +103,6 @@
 
     wbuf[0, 0:3 * HD, :] = wown[0:3 * HD, :]
 
-    pl.semaphore_wait(bar, 3 + 6 + 7 + jnp.where(is_root, 3, 4))
-
-    def w0_copy(k):
-        first, tiles = PIECES[k]
-        start = 0 if tiles == 3 else 3
-        return remote(
-            wown.at[pl.ds(start * HD, tiles * HD), :], w_rows(0, k), w0_send.at[k - 1], w_recv.at[0, k], z_at(k)
-        )
-
-    def h0_copy(match, plane, sub):
-        tiles, start = (3, 0) if match == 0 else (2, 3)
-        dst_side = lax.rem(x // 2 + match, 2)
-        dst_f = (pair * 2 + dst_side) * 2 + x % 2
-        rel = lax.rem(zh + pair, 2)
-        same = is_root & (side == dst_side) if plane == 0 else jnp.bool_(False)
-        first = rel * tiles + (0 if match == 0 else 6)
-        return jnp.logical_not(same), first, remote(
-            hid.at[pl.ds(start, tiles), pl.ds(sub * SUB, SUB), :],
-            hbuf.at[pl.ds(first, tiles), sub, pl.ds(own_tb * SUB, SUB), :],
-            h0_send.at[match, plane, sub],
-            hz_recv.at[rel, own_tb, sub],
-            (g, dst_f, (zh if plane == 0 else 1 - zh) * 4 + x),
-        )
-
-    def s_copy(k):
-        return remote(ssqb.at[t], ssqb.at[t], s_send.at[k - 1], s_recv.at[t], (g, f, lax.rem(t + k, 8)))
-
-    def w_rows(slot, p):
-        first, tiles = PIECES[p]
-        return wbuf.at[slot, pl.ds(first * HD, tiles * HD), :]
-
-    def y_copy(direction, k, p):
-        if direction == 0:
-            src, dst, dev = (8 - k) % 8, 7 - k, up
-        else:
-            src, dst, dev = k, k + 1, down
-        return remote(w_rows(src, p), w_rows(dst, p), y_send.at[direction, k, p], w_recv.at[dst, p], dev)
-
-    def y_goes(direction, k, p):
-        return k < 3 or p // 2 == direction
-
-    def w_wait(slot, p):
-        rows = w_rows(slot, p)
-        remote(rows, rows, y_send.at[0, 0, 0], w_recv.at[slot, p], up).wait_recv()
-
-    def hz_wait(match, rel, tb, sub):
-        tiles = 3 if match == 0 else 2
-        rows = hbuf.at[pl.ds((0 if match == 0 else 6) + rel * tiles, tiles), sub, pl.ds(tb * SUB, SUB), :]
-        remote(rows, rows, hx_send.at[0, 0, 0], hz_recv.at[rel, tb, sub], right).wait_recv()
-
-    def h_rows(match, tp, sub):
-        tiles = pl.ds(0, 6) if match == 0 else pl.ds(6, 4)
-        return hbuf.at[tiles, sub, pl.ds(tp * 2 * SUB, 2 * SUB), :]
-
-    def h_wait(match, tp, sub):
-        rows = h_rows(match, tp, sub)
-        remote(rows, rows, hx_send.at[0, 0, 0], hx_recv.at[match, tp, sub], right).wait_recv()
-
-    def hx_copy(match, tp, sub, direction):
-        rows = h_rows(match, tp, sub)
-        return remote(
-            rows, rows, hx_send.at[direction, tp, sub], hx_recv.at[match, tp, sub],
-            right if direction == 0 else left,
-        )
-
-    def start_y(k, p):
-        for direction in range(2):
-            if y_goes(direction, k, p):
-                y_copy(direction, k, p).start()
-
-    start_y(0, 0)
-    w0_copy(1).start()
-
     inputs[1].wait()
     inputs[2].wait()
     eye = lax.broadcasted_iota(jnp.int32, (ROWS, HD), 0) == lax.broadcasted_iota(jnp.int32, (ROWS, HD), 1)
@@ -193,105 +120,6 @@
             jnp.sum(jnp.where(eye, jnp.sum(squares, axis=1, keepdims=True), 0.0), axis=0, keepdims=True)
         )
     ssqb[t] = jnp.concatenate(ssq_rows + [jnp.zeros((8 - STEPS, HD), F32)], axis=0)
-
-    for sub in range(SUBS):
-        if sub == LATE:
-            w0_copy(2).start()
-            w0_copy(3).start()
-        for plane in (1, 0):
-            for match in range(2):
-                cond, first, copy = h0_copy(match, plane, sub)
-
-                @pl.when(cond)
-                def _():
-                    copy.start()
-
-    if LATE == SUBS:
-        w0_copy(2).start()
-        w0_copy(3).start()
-    for k in range(1, 8):
-        s_copy(k).start()
-
-    rel_own = lax.rem(zh + pair, 2)
-    for match in range(2):
-        tiles, start = (3, 0) if match == 0 else (2, 3)
-
-        @pl.when(is_root & (side == lax.rem(x // 2 + match, 2)))
-        def _():
-            for sub in range(SUBS):
-                for kt in range(tiles):
-                    hbuf[rel_own * tiles + (0 if match == 0 else 6) + kt, sub, pl.ds(own_tb * SUB, SUB), :] = hid[
-                        start + kt, sub * SUB:(sub + 1) * SUB, :
-                    ]
-
-    root_match = x // 2 == side
-    left_match = lax.rem(x + 3, 4) // 2 == side
-
-    def for_match(flag, body):
-        @pl.when(flag)
-        def _():
-            body(0)
-
-        @pl.when(jnp.logical_not(flag))
-        def _():
-            body(1)
-
-    def h_step(sub):
-        @pl.when(is_root)
-        def _():
-            def root(match):
-                for tp in range(2):
-                    for tb in (2 * tp, 2 * tp + 1):
-                        for rel in range(2):
-                            @pl.when(jnp.logical_not((rel_own == rel) & (own_tb == tb)))
-                            def _():
-                                hz_wait(match, rel, tb, sub)
-
-                    hx_copy(match, tp, sub, 0).start()
-                    hx_copy(match, tp, sub, 1).start()
-
-            for_match(root_match, root)
-
-        @pl.when(jnp.logical_not(is_root))
-        def _():
-            def passer(match):
-                h_wait(match, 0, sub)
-                hx_copy(match, 0, sub, 0).start()
-                h_wait(1 - match, 1, sub)
-                hx_copy(1 - match, 1, sub, 1).start()
-
-            for_match(left_match, passer)
-
-    def h_last(sub):
-        @pl.when(is_root)
-        def _():
-            def root(match):
-                for tp in range(2):
-                    h_wait(1 - match, tp, sub)
-
-            for_match(root_match, root)
-
-        @pl.when(jnp.logical_not(is_root))
-        def _():
-            def passer(match):
-                h_wait(match, 1, sub)
-                h_wait(1 - match, 0, sub)
-
-            for_match(left_match, passer)
-
-    def w_step(k, p):
-        w_wait(8 - k, p)
-        if y_goes(0, k, p):
-            y_copy(0, k, p).start()
-        w_wait(k, p)
-        if y_goes(1, k, p):
-            y_copy(1, k, p).start()
-
-    def w_first(p):
-        w_wait(0, p)
-        start_y(0, p)
-
-    w_first(1)
 
     inputs[3].wait()
     inputs[4].wait()
@@ -313,6 +141,178 @@
         chosen = jnp.sum(jnp.where(row_at == 4 * i + lane_at // 32, column, 0.0), axis=0, keepdims=True)
         last[i] = jnp.broadcast_to(chosen + (lane % STEPS - STEPS).astype(F32), (8, HD))
 
+    pl.semaphore_wait(bar, 3 + 6 + 7 + jnp.where(is_root, 3, 4))
+
+    def w0_copy(k):
+        first, tiles = PIECES[k]
+        start = 0 if tiles == 3 else 3
+        return remote(
+            wown.at[pl.ds(start * HD, tiles * HD), :], w_rows(0, k), w0_send.at[k - 1], w_recv.at[0, k], z_at(k)
+        )
+
+    def h0_copy(match, plane, sub):
+        tiles, start = (3, 0) if match == 0 else (2, 3)
+        dst_side = lax.rem(x // 2 + match, 2)
+        dst_f = (pair * 2 + dst_side) * 2 + x % 2
+        rel = lax.rem(zh + pair, 2)
+        same = is_root & (side == dst_side) if plane == 0 else jnp.bool_(False)
+        first = rel * tiles + (0 if match == 0 else 6)
+        return jnp.logical_not(same), first, remote(
+            hid.at[pl.ds(start, tiles), pl.ds(sub * SUB, SUB), :],
+            hbuf.at[pl.ds(first, tiles), sub, pl.ds(own_tb * SUB, SUB), :],
+            h0_send.at[match, plane, sub],
+            hz_recv.at[rel, own_tb, sub],
+            (g, dst_f, (zh if plane == 0 else 1 - zh) * 4 + x),
+        )
+
+    def s_copy(k):
+        return remote(ssqb.at[t], ssqb.at[t], s_send.at[k - 1], s_recv.at[t], (g, f, lax.rem(t + k, 8)))
+
+    def w_rows(slot, p):
+        first, tiles = PIECES[p]
+        return wbuf.at[slot, pl.ds(first * HD, tiles * HD), :]
+
+    def y_copy(direction, k, p):
+        if direction == 0:
+            src, dst, dev = (8 - k) % 8, 7 - k, up
+        else:
+            src, dst, dev = k, k + 1, down
+        return remote(w_rows(src, p), w_rows(dst, p), y_send.at[direction, k, p], w_recv.at[dst, p], dev)
+
+    def y_goes(direction, k, p):
+        return k < 3 or p // 2 == direction
+
+    def w_wait(slot, p):
+        rows = w_rows(slot, p)
+        remote(rows, rows, y_send.at[0, 0, 0], w_recv.at[slot, p], up).wait_recv()
+
+    def hz_wait(match, rel, tb, sub):
+        tiles = 3 if match == 0 else 2
+        rows = hbuf.at[pl.ds((0 if match == 0 else 6) + rel * tiles, tiles), sub, pl.ds(tb * SUB, SUB), :]
+        remote(rows, rows, hx_send.at[0, 0, 0], hz_recv.at[rel, tb, sub], right).wait_recv()
+
+    def h_rows(match, tp, sub):
+        tiles = pl.ds(0, 6) if match == 0 else pl.ds(6, 4)
+        return hbuf.at[tiles, sub, pl.ds(tp * 2 * SUB, 2 * SUB), :]
+
+    def h_wait(match, tp, sub):
+        rows = h_rows(match, tp, sub)
+        remote(rows, rows, hx_send.at[0, 0, 0], hx_recv.at[match, tp, sub], right).wait_recv()
+
+    def hx_copy(match, tp, sub, direction):
+        rows = h_rows(match, tp, sub)
+        return remote(
+            rows, rows, hx_send.at[direction, tp, sub], hx_recv.at[match, tp, sub],
+            right if direction == 0 else left,
+        )
+
+    def start_y(k, p):
+        for direction in range(2):
+            if y_goes(direction, k, p):
+                y_copy(direction, k, p).start()
+
+    start_y(0, 0)
+    w0_copy(1).start()
+
+    for sub in range(SUBS):
+        if sub == LATE:
+            w0_copy(2).start()
+            w0_copy(3).start()
+        for plane in (1, 0):
+            for match in range(2):
+                cond, first, copy = h0_copy(match, plane, sub)
+
+                @pl.when(cond)
+                def _():
+                    copy.start()
+
+    if LATE == SUBS:
+        w0_copy(2).start()
+        w0_copy(3).start()
+    for k in range(1, 8):
+        s_copy(k).start()
+
+    rel_own = lax.rem(zh + pair, 2)
+    for match in range(2):
+        tiles, start = (3, 0) if match == 0 else (2, 3)
+
+        @pl.when(is_root & (side == lax.rem(x // 2 + match, 2)))
+        def _():
+            for sub in range(SUBS):
+                for kt in range(tiles):
+                    hbuf[rel_own * tiles + (0 if match == 0 else 6) + kt, sub, pl.ds(own_tb * SUB, SUB), :] = hid[
+                        start + kt, sub * SUB:(sub + 1) * SUB, :
+                    ]
+
+    root_match = x // 2 == side
+    left_match = lax.rem(x + 3, 4) // 2 == side
+
+    def for_match(flag, body):
+        @pl.when(flag)
+        def _():
+            body(0)
+
+        @pl.when(jnp.logical_not(flag))
+        def _():
+            body(1)
+
+    def h_step(sub):
+        @pl.when(is_root)
+        def _():
+            def root(match):
+                for tp in range(2):
+                    for tb in (2 * tp, 2 * tp + 1):
+                        for rel in range(2):
+                            @pl.when(jnp.logical_not((rel_own == rel) & (own_tb == tb)))
+                            def _():
+                                hz_wait(match, rel, tb, sub)
+
+                    hx_copy(match, tp, sub, 0).start()
+                    hx_copy(match, tp, sub, 1).start()
+
+            for_match(root_match, root)
+
+        @pl.when(jnp.logical_not(is_root))
+        def _():
+            def passer(match):
+                h_wait(match, 0, sub)
+                hx_copy(match, 0, sub, 0).start()
+                h_wait(1 - match, 1, sub)
+                hx_copy(1 - match, 1, sub, 1).start()
+
+            for_match(left_match, passer)
+
+    def h_last(sub):
+        @pl.when(is_root)
+        def _():
+            def root(match):
+                for tp in range(2):
+                    h_wait(1 - match, tp, sub)
+
+            for_match(root_match, root)
+
+        @pl.when(jnp.logical_not(is_root))
+        def _():
+            def passer(match):
+                h_wait(match, 1, sub)
+                h_wait(1 - match, 0, sub)
+
+            for_match(left_match, passer)
+
+    def w_step(k, p):
+        w_wait(8 - k, p)
+        if y_goes(0, k, p):
+            y_copy(0, k, p).start()
+        w_wait(k, p)
+        if y_goes(1, k, p):
+            y_copy(1, k, p).start()
+
+    def w_first(p):
+        w_wait(0, p)
+        start_y(0, p)
+
+    w_first(1)
+
     w_step(1, 0)
     w_step(1, 1)
     h_step(0)
@@ -321,9 +321,9 @@
     h_step(1)
     w_first(2)
     w_first(3)
+    h_step(2)
     w_step(3, 0)
     w_step(3, 1)
-    h_step(2)
     w_step(1, 2)
     w_step(1, 3)
     h_step(3)

time: 71.2 us -> 70 us (0.983)
  the two profiles are of different devices: /device:TPU:2 before, /device:TPU:6 now
where the time goes in v4:
time: 70 us; the launch traced here: 69.9 us
  Pallas kernels  68 us (97%)
  local copies, waits for them, and re-layouts  1.88 us (3%)
    pallas_call x1, Pallas kernels, shards(): call(hidden_in, norm_gain, master_query.reshape(KB, HD), query_gain, leng...  68 us
    unnamed x1, local copies, waits for them, and re-layouts  1.88 us

profile of v4, /device:TPU:6, one launch (start us, length us, event | category | flops | bytes accessed | tf_op | source)
XLA Modules:
  0.0 69.9 jit_solution(15806574290594283390)
XLA Ops:
  0.0 68.0 %shard_map.64 = bf16[48,32,128]{2,1,0:T(8,128)(2,1)} custom-call(bf16[48,4,640]{2,1,0:T(4,128)(2,1)} %hid_in.1, bf16[640]{0:T(1024)(128)(2,1)} %gain_in.1, f32[640,128]{1,0:T(8,128)} %bitcast.9, f32[128]{0:T(128)} %qgain_in.1, s32[48]{0:T(128)} %lens_in.1, bf16[48,128,256]{2,1,0:T(8,128)(2,1)} %bitcast.7), custom_call_target="tpu_custom_call" | custom-call | tf_op jit(solution)/shard_map/pallas_call | solution.py:588
  68.0 1.9 %copy.9 = bf16[48,4,1024]{2,1,0:T(4,128)(2,1)} copy(bf16[48,4,1024]{2,1,0:T(4,128)(2,1)} %bitcast.8) | data formatting | bytes 786432

commit v5 on v4

--- a/solution.py
+++ b/solution.py
@@ -484,16 +484,16 @@
     multiply(1, 1)
     multiply(1, 2)
     second(0, 2)
-    early_sent()
+    second(1, 0)
+    second(1, 1)
     for p in range(4):
         w_wait(4, p)
     multiply4()
-    second(1, 0)
-    second(1, 1)
     second(1, 2)
     second4()
     third(0)
     third(1)
+    early_sent()
     third4()
 
     inputs[5].wait()

time: 70 us -> 70 us (level)
  no operation moved by 1% of the time
where the time goes in v5:
time: 70 us; the launch traced here: 69.8 us
  Pallas kernels  67.9 us (97%)
  local copies, waits for them, and re-layouts  1.88 us (3%)
    pallas_call x1, Pallas kernels, shards(): call(hidden_in, norm_gain, master_query.reshape(KB, HD), query_gain, leng...  67.9 us
    unnamed x1, local copies, waits for them, and re-layouts  1.88 us

profile of v5, /device:TPU:6, one launch (start us, length us, event | category | flops | bytes accessed | tf_op | source)
XLA Modules:
  0.0 69.8 jit_solution(13796741237291230684)
XLA Ops:
  0.0 67.9 %shard_map.64 = bf16[48,32,128]{2,1,0:T(8,128)(2,1)} custom-call(bf16[48,4,640]{2,1,0:T(4,128)(2,1)} %hid_in.1, bf16[640]{0:T(1024)(128)(2,1)} %gain_in.1, f32[640,128]{1,0:T(8,128)} %bitcast.9, f32[128]{0:T(128)} %qgain_in.1, s32[48]{0:T(128)} %lens_in.1, bf16[48,128,256]{2,1,0:T(8,128)(2,1)} %bitcast.7), custom_call_target="tpu_custom_call" | custom-call | tf_op jit(solution)/shard_map/pallas_call | solution.py:588
  68.0 1.9 %copy.9 = bf16[48,4,1024]{2,1,0:T(4,128)(2,1)} copy(bf16[48,4,1024]{2,1,0:T(4,128)(2,1)} %bitcast.8) | data formatting | bytes 786432
